TPU v7x, 32 devices: a whole 2x2x4 slice. The times are simulated.
32 devices in a mesh: blk: 8 (over y, x, core), uly: 4 (over z).
Axes of the slice: x: 2, y: 2, z: 4, core: 2. Of those that a mesh axis runs over, the one named last changes fastest.
Arguments:
- activations: bfloat16 [3072, 4096], P(('blk', 'uly')), may hold values from -64 to 64
- input_norm_gain: float32 [4096], replicated, may hold values from 0.5 to 2
- query_weight: bfloat16 [4096, 4096], P(None, 'uly'), may hold values from -3 to 3
- key_weight: bfloat16 [4096, 1024], P(None, 'uly'), may hold values from -3 to 3
- value_weight: bfloat16 [4096, 1024], P(None, 'uly'), may hold values from -0.09375 to 0.09375
- output_weight: bfloat16 [4096, 4096], P('uly'), may hold values from -1 to 1
- adapter_down_maps: bfloat16 [4096, 384], replicated, may hold values from -0.09375 to 0.09375
- query_up_maps: bfloat16 [128, 4096], P(None, 'uly'), may hold values from -0.375 to 0.375
- key_up_maps: bfloat16 [128, 1024], P(None, 'uly'), may hold values from -0.375 to 0.375
- value_up_maps: bfloat16 [128, 1024], P(None, 'uly'), may hold values from -0.375 to 0.375
- output_down_maps: bfloat16 [4096, 128], P('uly'), may hold values from -0.5 to 0.5
- output_up_maps: bfloat16 [128, 4096], replicated, may hold values from -1.5 to 1.5
- segment_index: int32 [3072], replicated, may hold values from 0 to 3, never falling along the last dimension, each value on 1 to 2304 neighbouring positions
- segment_adapter: int32 [4], replicated, may hold values from 0 to 7
Outputs:
- attn_out: bfloat16 [3072, 4096], P(('blk', 'uly'))
Inputs may be any that keep to these rules, and one draw needn't show every extreme that they name: `segment_index`: never falling along the sequence; each of the 4 segments covers 1 to 2304 tokens, and one covers exactly that many. `segment_adapter`: one adapter per segment; segments may share one.
All inputs are finite; a program needn't handle non-finite values.
Results may differ from a plain program's by a relative error of at most 0.019.
The roundings to bfloat16 on the way count: a program that leaves them out, or rounds other values in their place, can miss the bound.
Values may be sent and summed in bfloat16 or wider, within the bound.
A program may use at most 192 MiB of HBM per device.

v0:
```python
import math

import jax
import jax.numpy as jnp
from jax import lax
from jax.sharding import PartitionSpec as P

QUERY_HEADS = 32
KEY_VALUE_HEADS = 8
HEAD_SIZE = 128
ADAPTER_RANK = 16
ADAPTER_COUNT = 8


eps_norm = 1e-05
adapter_scale = 2.0


def tenant_rows(seg_rows, segment_adapter):
    match = seg_rows[:, None] == jnp.arange(segment_adapter.shape[0], dtype=jnp.int32)[None, :]
    return jnp.sum(jnp.where(match, segment_adapter[None, :], 0), axis=1)


def normalize(activations, input_norm_gain):
    values = activations.astype(jnp.float32)
    power = jnp.mean(values * values, axis=1, keepdims=True)
    return (values * lax.rsqrt(power + eps_norm) * input_norm_gain[None, :]).astype(jnp.bfloat16)


def tenant_adapter_mask(tenant_index, hidden_width):
    columns = jnp.arange(hidden_width, dtype=jnp.int32) // ADAPTER_RANK % ADAPTER_COUNT
    return columns[None, :] == tenant_index[:, None]


def attend_local(query_rows, key_matrix_rows, value_matrix_rows, query_pos, segment_index):
    total_rows = query_rows.shape[0]
    kv_heads = key_matrix_rows.shape[1] // HEAD_SIZE
    query_group = QUERY_HEADS // KEY_VALUE_HEADS
    score_scale = 1.0 / math.sqrt(HEAD_SIZE)
    query_matrix = query_rows.reshape(total_rows, kv_heads, query_group, HEAD_SIZE)
    query_seg = jnp.take(segment_index, query_pos)
    last_query = jnp.max(query_pos)
    init = (
        jnp.full((total_rows, kv_heads, query_group), -1e30, jnp.float32),
        jnp.zeros((total_rows, kv_heads, query_group), jnp.float32),
        jnp.zeros((total_rows, kv_heads, query_group, HEAD_SIZE), jnp.float32),
    )
    key_piece = lax.all_gather(key_matrix_rows, "blk", axis=0, tiled=True)
    value_piece = lax.all_gather(value_matrix_rows, "blk", axis=0, tiled=True)
    count = key_piece.shape[0]
    step = math.gcd(count, 512)

    def visit(index, state):
        offset = index * step

        def compute(inner):
            peak, total, summed = inner
            key_block = lax.dynamic_slice_in_dim(key_piece, offset, step).reshape(
                step, kv_heads, HEAD_SIZE
            )
            value_block = lax.dynamic_slice_in_dim(value_piece, offset, step).reshape(
                step, kv_heads, HEAD_SIZE
            )
            key_pos = offset + jnp.arange(step, dtype=jnp.int32)
            key_seg = lax.dynamic_slice_in_dim(segment_index, offset, step)
            allowed = (key_pos[None, :] <= query_pos[:, None]) & (
                key_seg[None, :] == query_seg[:, None]
            )
            allowed = allowed[:, None, None, :]
            scores = (
                jnp.einsum(
                    "rkgd,nkd->rkgn", query_matrix, key_block, preferred_element_type=jnp.float32
                )
                * score_scale
            )
            fresh = jnp.maximum(peak, jnp.max(jnp.where(allowed, scores, -1e30), axis=3))
            weights = jnp.where(allowed, jnp.exp(scores - fresh[..., None]), 0.0)
            decay = jnp.exp(peak - fresh)
            total = total * decay + jnp.sum(weights, axis=3)
            summed = summed * decay[..., None] + jnp.einsum(
                "rkgn,nkd->rkgd",
                weights.astype(jnp.bfloat16),
                value_block,
                preferred_element_type=jnp.float32,
            )
            return (fresh, total, summed)

        return lax.cond(offset <= last_query, compute, lambda inner: inner, state)

    peak, total, summed = lax.fori_loop(0, count // step, visit, init)
    return (
        (summed / total[..., None])
        .reshape(total_rows, kv_heads * query_group * HEAD_SIZE)
        .astype(jnp.bfloat16)
    )


def shards(
    activations,
    input_norm_gain,
    query_weight,
    key_weight,
    value_weight,
    output_weight,
    adapter_down_maps,
    query_up_maps,
    key_up_maps,
    value_up_maps,
    output_down_maps,
    output_up_maps,
    segment_index,
    segment_adapter,
):
    rows = activations.shape[0]
    features = activations.shape[1]
    head_split = lax.axis_size("uly")
    block_index = lax.axis_index("blk")
    head_index = lax.axis_index("uly")
    block_rows = rows * head_split
    block_start = block_index * block_rows
    own_start = block_start + head_index * rows
    hidden_width = ADAPTER_COUNT * ADAPTER_RANK
    tenant_index = tenant_rows(
        lax.dynamic_slice_in_dim(segment_index, own_start, rows), segment_adapter
    )
    normed_input = normalize(activations, input_norm_gain)
    lowered_rows = jnp.where(
        tenant_adapter_mask(tenant_index, 3 * hidden_width),
        jnp.dot(normed_input, adapter_down_maps, preferred_element_type=jnp.float32),
        0.0,
    ).astype(jnp.bfloat16)
    packed = jnp.concatenate([normed_input, lowered_rows], axis=1)
    piece = lax.all_gather(packed, "uly", axis=0, tiled=True)
    input_rows = piece[:, :features]
    rank_rows = piece[:, features:]
    query_part = jnp.dot(
        input_rows, query_weight, preferred_element_type=jnp.float32
    ) + adapter_scale * jnp.dot(
        rank_rows[:, :hidden_width], query_up_maps, preferred_element_type=jnp.float32
    )
    key_portion = jnp.dot(
        input_rows, key_weight, preferred_element_type=jnp.float32
    ) + adapter_scale * jnp.dot(
        rank_rows[:, hidden_width : 2 * hidden_width],
        key_up_maps,
        preferred_element_type=jnp.float32,
    )
    value_part = jnp.dot(
        input_rows, value_weight, preferred_element_type=jnp.float32
    ) + adapter_scale * jnp.dot(
        rank_rows[:, 2 * hidden_width :], value_up_maps, preferred_element_type=jnp.float32
    )
    projected = jnp.concatenate([query_part, key_portion, value_part], axis=1).astype(jnp.bfloat16)
    query_width = query_weight.shape[1]
    key_width = key_weight.shape[1]
    query_rows = projected[:, :query_width]
    key_matrix_rows = projected[:, query_width : query_width + key_width]
    value_matrix_rows = projected[:, query_width + key_width :]
    offsets = jnp.arange(block_rows, dtype=jnp.int32)
    query_pos = block_start + offsets
    mixed_heads = attend_local(
        query_rows, key_matrix_rows, value_matrix_rows, query_pos, segment_index
    )
    output_up_rows = output_up_maps.astype(jnp.float32)
    block_tenant = tenant_rows(
        lax.dynamic_slice_in_dim(segment_index, block_start, block_rows), segment_adapter
    )
    segment_block_mask = tenant_adapter_mask(block_tenant, hidden_width)
    lows_part = jnp.where(
        segment_block_mask,
        jnp.dot(mixed_heads, output_down_maps, preferred_element_type=jnp.float32),
        0.0,
    )
    summed = lax.psum_scatter(
        jnp.concatenate(
            [jnp.dot(mixed_heads, output_weight, preferred_element_type=jnp.float32), lows_part],
            axis=1,
        ).astype(jnp.bfloat16),
        "uly",
        scatter_dimension=0,
        tiled=True,
    ).astype(jnp.float32)
    main_entry = summed[:, :features]
    rank_rows = summed[:, features:]
    block_result = main_entry + adapter_scale * jnp.dot(
        rank_rows, output_up_rows, precision=lax.Precision.HIGHEST
    )
    return block_result.astype(jnp.bfloat16)


def solution(mesh):
    return jax.shard_map(
        shards,
        mesh=mesh,
        in_specs=(
            P(("blk", "uly"), None),
            P(),
            P(None, "uly"),
            P(None, "uly"),
            P(None, "uly"),
            P("uly", None),
            P(),
            P(None, "uly"),
            P(None, "uly"),
            P(None, "uly"),
            P("uly", None),
            P(),
            P(),
            P(),
        ),
        out_specs=P(("blk", "uly"), None),
        check_vma=False,
    )
```

profile of v0, /device:TPU:15, one launch (start us, length us, event | category | flops | bytes accessed | tf_op | source)
XLA Modules:
  0.0 280.0 jit_solution(8907900385493180227)
XLA Ops:
  6.5 1.5 fusion.25
  8.1 2.3 fusion.27
  10.4 0.8 dynamic_slice.15
  11.2 0.7 select_reduce_fusion.1
  12.0 1.8 fusion.33
  13.8 1.0 pad_maximum_fusion.1
  14.8 67.1 %all-gather.4.cloned.1.call-done = bf16[384,4480]{1,0:T(8,128)(2,1)} async-done(((bf16[96,4480]{1,0:T(8,128)(2,1)}), bf16[384,4480]{1,0:T(8,128)(2,1)}) %all-gather.4.cloned.1.call-update) | async-done | bytes 3440656 | tf_op jit(solution)/shard_map/all_gather | solution.py:133
  82.0 3.5 %fusion.23 = f32[384,256]{1,0:T(8,128)S(1)} fusion(bf16[4096,256]{1,0:T(8,128)(2,1)} %param.21, bf16[384,4480]{1,0:T(8,128)(2,1)} %all-gather.4.cloned.1.call-done), kind=kOutput, calls=%fused_computation.33 | convolution fusion | flops 805306368 | bytes 5636096 | tf_op jit(solution)/shard_map/dot_general | solution.py:141
  85.5 1.8 fusion.31
  87.4 3.5 %fusion.19 = f32[384,256]{1,0:T(8,128)S(1)} fusion(bf16[4096,256]{1,0:T(8,128)(2,1)} %param.22, bf16[384,4480]{1,0:T(8,128)(2,1)} %all-gather.4.cloned.1.call-done), kind=kOutput, calls=%fused_computation.29 | convolution fusion | flops 805306368 | bytes 5636096 | tf_op jit(solution)/shard_map/dot_general | solution.py:148
  91.0 1.8 fusion.30
  92.8 2.5 gather_fusion
  95.6 0.6 fusion.41
  96.2 6.9 %fusion.21 = f32[384,1024]{1,0:T(8,128)S(1)} fusion(bf16[4096,1024]{1,0:T(8,128)(2,1)} %param.20, bf16[384,4480]{1,0:T(8,128)(2,1)} %all-gather.4.cloned.1.call-done), kind=kOutput, calls=%fused_computation.31 | convolution fusion | flops 3221225472 | bytes 13107200 | tf_op jit(solution)/shard_map/dot_general | solution.py:136
  103.1 2.1 add_convert_fusion
  105.2 2.6 reshape.148
  107.8 2.1 copy.28
  110.0 3.7 %all-gather.6.cloned.1.call-done = bf16[3072,256]{1,0:T(8,128)(2,1)} async-done(((bf16[384,256]{1,0:T(8,128)(2,1)}), bf16[3072,256]{1,0:T(8,128)(2,1)}) %all-gather.6.cloned.1.call-update) | async-done | bytes 1572880 | tf_op jit(solution)/shard_map/all_gather | solution.py:48
  113.7 2.6 copy.27
  116.3 25.0 %all-gather.8.cloned.1.call-done = bf16[3072,256]{1,0:T(8,128)(2,1)} async-done(((bf16[384,256]{1,0:T(8,128)(2,1)}), bf16[3072,256]{1,0:T(8,128)(2,1)}) %all-gather.8.cloned.1.call-update) | async-done | bytes 1572880 | tf_op jit(solution)/shard_map/all_gather | solution.py:49
  141.3 2.6 copy.29
  143.9 1.3 broadcast_in_dim.87
  145.2 52.7 %while.18 = (s32[]{:T(128)}, f32[384,2,4]{0,2,1:T(4,128)S(1)}, f32[384,2,4]{0,2,1:T(4,128)S(1)}, f32[384,2,4,128]{0,3,2,1:T(8,128)}, s32[]{:T(128)}, /*index=5*/...) while((s32[]{:T(128)}, f32[384,2,4]{0,2,1:T(4,128)S(1)}, ...), condition=%wide.region_8.9_spmd.clone, body=%wide.region_3.8_spmd.clone.sunk | while | flops 823991168 | bytes 37963672 | solution.py:90
  145.8 8.2 %conditional.3 = ((f32[384,2,4]{0,2,1:T(4,128)S(1)}, f32[384,2,4]{0,2,1:T(4,128)S(1)}, f32[384,2,4,128]{0,3,2,1:T(8,128)})) conditional(s32[]{:T(128)} %convert_element_type.56, (f32[384,2,4]{0,2,1:T(4,128)S(1)}, f32[384,2,4]{0,2,1:T(4,128)S(1)}, f32[384,2,4,128]{0,3,2,1:T(8,128)}) %tuple.50, (s32[]{:T(128)}, s32[]{:T(128)}, s32[3072]{0:T(1024)S(1)}, ...), branch_computations={%region_4.4_spmd, %region_5.7_spmd} | conditional | flops 823991168 | bytes 37961864 | solution.py:88
  146.1 1.1 constant_dynamic-slice_fusion
  147.2 2.4 fusion.2
  149.6 1.3 fusion.6
  151.0 1.8 bitcast_add_fusion
  152.8 1.1 copy-done.4
  154.6 8.2 %conditional.3 = ((f32[384,2,4]{0,2,1:T(4,128)S(1)}, f32[384,2,4]{0,2,1:T(4,128)S(1)}, f32[384,2,4,128]{0,3,2,1:T(8,128)})) conditional(s32[]{:T(128)} %convert_element_type.56, (f32[384,2,4]{0,2,1:T(4,128)S(1)}, f32[384,2,4]{0,2,1:T(4,128)S(1)}, f32[384,2,4,128]{0,3,2,1:T(8,128)}) %tuple.50, (s32[]{:T(128)}, s32[]{:T(128)}, s32[3072]{0:T(1024)S(1)}, ...), branch_computations={%region_4.4_spmd, %region_5.7_spmd} | conditional | flops 823991168 | bytes 37961864 | solution.py:88
  154.9 1.1 constant_dynamic-slice_fusion
  156.0 2.4 fusion.2
  158.4 1.3 fusion.6
  159.8 1.8 bitcast_add_fusion
  161.6 1.1 copy-done.4
  163.3 8.2 %conditional.3 = ((f32[384,2,4]{0,2,1:T(4,128)S(1)}, f32[384,2,4]{0,2,1:T(4,128)S(1)}, f32[384,2,4,128]{0,3,2,1:T(8,128)})) conditional(s32[]{:T(128)} %convert_element_type.56, (f32[384,2,4]{0,2,1:T(4,128)S(1)}, f32[384,2,4]{0,2,1:T(4,128)S(1)}, f32[384,2,4,128]{0,3,2,1:T(8,128)}) %tuple.50, (s32[]{:T(128)}, s32[]{:T(128)}, s32[3072]{0:T(1024)S(1)}, ...), branch_computations={%region_4.4_spmd, %region_5.7_spmd} | conditional | flops 823991168 | bytes 37961864 | solution.py:88
  163.7 1.1 constant_dynamic-slice_fusion
  164.8 2.4 fusion.2
  167.2 1.3 fusion.6
  168.6 1.8 bitcast_add_fusion
  170.4 1.1 copy-done.4
  172.1 8.2 %conditional.3 = ((f32[384,2,4]{0,2,1:T(4,128)S(1)}, f32[384,2,4]{0,2,1:T(4,128)S(1)}, f32[384,2,4,128]{0,3,2,1:T(8,128)})) conditional(s32[]{:T(128)} %convert_element_type.56, (f32[384,2,4]{0,2,1:T(4,128)S(1)}, f32[384,2,4]{0,2,1:T(4,128)S(1)}, f32[384,2,4,128]{0,3,2,1:T(8,128)}) %tuple.50, (s32[]{:T(128)}, s32[]{:T(128)}, s32[3072]{0:T(1024)S(1)}, ...), branch_computations={%region_4.4_spmd, %region_5.7_spmd} | conditional | flops 823991168 | bytes 37961864 | solution.py:88
  172.5 1.1 constant_dynamic-slice_fusion
  173.6 2.4 fusion.2
  176.0 1.3 fusion.6
  177.4 1.8 bitcast_add_fusion
  179.2 1.1 copy-done.4
  180.9 8.2 %conditional.3 = ((f32[384,2,4]{0,2,1:T(4,128)S(1)}, f32[384,2,4]{0,2,1:T(4,128)S(1)}, f32[384,2,4,128]{0,3,2,1:T(8,128)})) conditional(s32[]{:T(128)} %convert_element_type.56, (f32[384,2,4]{0,2,1:T(4,128)S(1)}, f32[384,2,4]{0,2,1:T(4,128)S(1)}, f32[384,2,4,128]{0,3,2,1:T(8,128)}) %tuple.50, (s32[]{:T(128)}, s32[]{:T(128)}, s32[3072]{0:T(1024)S(1)}, ...), branch_computations={%region_4.4_spmd, %region_5.7_spmd} | conditional | flops 823991168 | bytes 37961864 | solution.py:88
  181.2 1.1 constant_dynamic-slice_fusion
  182.3 2.4 fusion.2
  184.7 1.3 fusion.6
  186.1 1.8 bitcast_add_fusion
  187.9 1.1 copy-done.4
  189.7 8.2 %conditional.3 = ((f32[384,2,4]{0,2,1:T(4,128)S(1)}, f32[384,2,4]{0,2,1:T(4,128)S(1)}, f32[384,2,4,128]{0,3,2,1:T(8,128)})) conditional(s32[]{:T(128)} %convert_element_type.56, (f32[384,2,4]{0,2,1:T(4,128)S(1)}, f32[384,2,4]{0,2,1:T(4,128)S(1)}, f32[384,2,4,128]{0,3,2,1:T(8,128)}) %tuple.50, (s32[]{:T(128)}, s32[]{:T(128)}, s32[3072]{0:T(1024)S(1)}, ...), branch_computations={%region_4.4_spmd, %region_5.7_spmd} | conditional | flops 823991168 | bytes 37961864 | solution.py:88
  190.0 1.1 constant_dynamic-slice_fusion
  191.1 2.4 fusion.2
  193.5 1.3 fusion.6
  194.9 1.8 bitcast_add_fusion
  196.7 1.1 copy-done.4
  197.9 1.5 divide_convert_fusion
  199.4 6.9 %convolution_convert_fusion = bf16[384,4096]{1,0:T(8,128)(2,1)S(1)} fusion(bf16[384,1024]{0,1:T(8,128)(2,1)S(1)} %bitcast.56, bf16[1024,4096]{1,0:T(8,128)(2,1)} %param.23), kind=kOutput, calls=%fused_computation.24 | convolution fusion | flops 3222798336 | bytes 12320768 | tf_op jit(solution)/shard_map/dot_general | solution.py:176
  206.8 1.9 pad_maximum_fusion
  208.7 62.0 %reduce-scatter.2.cloned.1.call-done = bf16[96,4224]{1,0:T(8,128)(2,1)} async-done(((bf16[384,4224]{1,0:T(8,128)(2,1)}), bf16[96,4224]{1,0:T(8,128)(2,1)}) %reduce-scatter.2.cloned.1.call-update) | async-done | bytes 811024 | tf_op jit(solution)/shard_map/reduce_scatter | solution.py:174
  270.8 2.7 fusion.18
  (100 shorter events, 3.3 us)
Async XLA Ops:
  6.5 5.4 %copy-start = (bf16[4096,384]{1,0:T(8,128)(2,1)S(1)}, bf16[4096,384]{1,0:T(8,128)(2,1)}, u32[]{:S(2)}) copy-start(bf16[4096,384]{1,0:T(8,128)(2,1)} %param.24) | copy-start | bytes 9437188
  6.5 75.4 %all-gather.4.cloned.1.call-start = ((), (), s32[]{:S(2)}) async-start(), calls=%async_computation.1 | async-start | bytes 4300800 | tf_op jit(solution)/shard_map/all_gather | solution.py:133
  10.4 3.4 %copy-start.2 = (bf16[96,4096]{1,0:T(8,128)(2,1)S(1)}, bf16[96,4096]{1,0:T(8,128)(2,1)}, u32[]{:S(2)}) copy-start(bf16[96,4096]{1,0:T(8,128)(2,1)} %fusion.27) | copy-start | bytes 2359300
  14.8 70.7 %copy-start.6 = (bf16[128,256]{1,0:T(8,128)(2,1)S(1)}, bf16[128,256]{1,0:T(8,128)(2,1)}, u32[]{:S(2)}) copy-start(bf16[128,256]{1,0:T(8,128)(2,1)} %param.26) | copy-start | bytes 196612
  14.8 98.9 %all-gather.6.cloned.1.call-start = ((), (), s32[]{:S(2)}) async-start(), calls=%async_computation.2 | async-start | bytes 1769472 | tf_op jit(solution)/shard_map/all_gather | solution.py:48
  87.3 3.6 %copy-start.7 = (bf16[128,256]{1,0:T(8,128)(2,1)S(1)}, bf16[128,256]{1,0:T(8,128)(2,1)}, u32[]{:S(2)}) copy-start(bf16[128,256]{1,0:T(8,128)(2,1)} %param.27) | copy-start | bytes 196612
  87.3 5.5 %copy-start.1 = (s32[3072]{0:T(1024)S(1)}, s32[3072]{0:T(1024)}, u32[]{:S(2)}) copy-start(s32[3072]{0:T(1024)} %param.30) | copy-start | bytes 36868
  87.3 8.1 %copy-start.8 = (s32[4]{0:T(128)S(1)}, s32[4]{0:T(128)}, u32[]{:S(2)}) copy-start(s32[4]{0:T(128)} %param.31) | copy-start | bytes 52
  87.4 54.0 %all-gather.8.cloned.1.call-start = ((), (), s32[]{:S(2)}) async-start(), calls=%async_computation.3 | async-start | bytes 1769472 | tf_op jit(solution)/shard_map/all_gather | solution.py:49
  92.7 178.0 %reduce-scatter.2.cloned.1.call-start = ((), (), s32[]{:S(2)}) async-start(), calls=%async_computation.4 | async-start | bytes 4055040 | tf_op jit(solution)/shard_map/reduce_scatter | solution.py:174
  96.2 6.9 %copy-start.5 = (bf16[128,1024]{1,0:T(8,128)(2,1)S(1)}, bf16[128,1024]{1,0:T(8,128)(2,1)}, u32[]{:S(2)}) copy-start(bf16[128,1024]{1,0:T(8,128)(2,1)} %param.25) | copy-start | bytes 786436
  149.6 1.4 copy-start.3
  152.8 1.2 copy-start.4
  158.4 1.4 copy-start.3
  161.6 1.2 copy-start.4
  167.2 1.4 copy-start.3
  170.4 1.2 copy-start.4
  176.0 1.4 copy-start.3
  179.1 1.2 copy-start.4
  184.7 1.4 copy-start.3
  187.9 1.2 copy-start.4
  193.5 1.4 copy-start.3
  196.7 1.2 copy-start.4
  199.4 6.9 %copy-start.9 = (bf16[1024,128]{1,0:T(8,128)(2,1)S(1)}, bf16[1024,128]{1,0:T(8,128)(2,1)}, u32[]{:S(2)}) copy-start(bf16[1024,128]{1,0:T(8,128)(2,1)} %param.28) | copy-start | bytes 786436
Sparse Core Ops, SparseCore 0:
  14.9 67.0 all-gather.3
  87.4 26.2 all-gather.5
  115.6 25.6 all-gather.7
  208.8 61.8 reduce-scatter.1
where the time goes:
time: 283 us; the launch traced here: 280 us
  waiting for transfers between devices  158 us (56%)
  matrix products  56.4 us (20%)
  local copies, waits for them, and re-layouts  29 us (10%)
  other arithmetic  19.1 us (7%)
  between operations  13.3 us (5%)
  loops' own time  4.12 us (1%)
    all_gather x1, waiting for transfers between devices, shards(): piece = lax.all_gather(packed, 'uly', axis=0, tiled=True)  67.1 us
    reduce_scatter x1, waiting for transfers between devices, shards(): lax.psum_scatter(jnp.concatenate([jnp.dot(mixed_heads, output_weight, pre...  62 us
    all_gather x1, waiting for transfers between devices, attend_local(): value_piece = lax.all_gather(value_matrix_rows, 'blk', axis=0, tiled=True)  25 us
    dot_general x6, matrix products, compute(): jnp.einsum('rkgd,nkd->rkgn', query_matrix, key_block, preferred_element_t...  14.3 us
    dot_general x6, matrix products, compute(): jnp.einsum('rkgn,nkd->rkgd', weights.astype(jnp.bfloat16), value_block, p...  10.7 us
    reduce_sum x6, other arithmetic, compute(): total = total * decay + jnp.sum(weights, axis=3)  7.81 us
    unnamed x19, local copies, waits for them, and re-layouts  7.34 us
    cond x30, local copies, waits for them, and re-layouts  7.33 us
  transfers between devices with their start and end apart: 4, of which 4 were waited for; matrix products, arithmetic and copies ran while one was open for 9% of the time, Pallas kernels for 0%

commit v1 on v0

v1 whole, which is shorter than its diff:
```python
import functools
import math

import jax
import jax.numpy as jnp
from jax import lax
from jax.experimental import pallas as pl
from jax.experimental.pallas import tpu as pltpu
from jax.sharding import PartitionSpec as P

QUERY_HEADS = 32
KEY_VALUE_HEADS = 8
HEAD_SIZE = 128
ADAPTER_RANK = 16
ADAPTER_COUNT = 8
HIDDEN = ADAPTER_COUNT * ADAPTER_RANK

eps_norm = 1e-05
adapter_scale = 2.0
MESH = pl.DeviceIdType.MESH
VMEM_LIMIT = 60 * 1024 * 1024
MASKED = -1e30


def segment_starts(seg_ref, segments):
    seg = seg_ref[...]
    starts = []
    for k in range(segments):
        below = jnp.where(seg < k, 1.0, 0.0)
        starts.append(jnp.sum(jnp.sum(below, axis=1, keepdims=True), axis=0, keepdims=True))
    return starts


def tenant_mask(starts, adapter_ref, first, rows, width):
    pos = (first + lax.broadcasted_iota(jnp.int32, (rows, width), 0)).astype(jnp.float32)
    column = lax.broadcasted_iota(jnp.int32, (rows, width), 1)
    column = (column // ADAPTER_RANK) % ADAPTER_COUNT
    tenant = jnp.zeros((rows, width), jnp.int32) + adapter_ref[0]
    for k in range(1, len(starts)):
        tenant = jnp.where(pos >= starts[k], adapter_ref[k], tenant)
    return column == tenant


def gather_kernel(
    H, B, C, segments,
    x_ref, gain_ref, down_ref, wq_ref, wk_ref, wv_ref, uq_ref, uk_ref, uv_ref, seg_ref, adapter_ref,
    q_ref, kv_ref,
    rows_buf, weights, kv_buf, w_sem, send_sem, recv_sem, kv_send, kv_recv, kv_local,
):
    u = lax.axis_index("uly")
    b = lax.axis_index("blk")
    rows = x_ref.shape[0]
    part = rows // C
    kw = wk_ref.shape[1]
    qw = wq_ref.shape[1]

    def weight_copies():
        return [
            pltpu.make_async_copy(wk_ref, weights.at[:, pl.ds(0, kw)], w_sem.at[0]),
            pltpu.make_async_copy(wv_ref, weights.at[:, pl.ds(kw, kw)], w_sem.at[1]),
            pltpu.make_async_copy(wq_ref, weights.at[:, pl.ds(2 * kw, qw)], w_sem.at[2]),
        ]

    for copy in weight_copies():
        copy.start()

    barrier = pltpu.get_barrier_semaphore()

    @pl.when(u > 0)
    def _():
        pl.semaphore_signal(barrier, inc=1, device_id=(b, u - 1), device_id_type=MESH)

    @pl.when(u < H - 1)
    def _():
        pl.semaphore_signal(barrier, inc=1, device_id=(b, u + 1), device_id_type=MESH)

    for d in range(1, B):
        pl.semaphore_signal(
            barrier, inc=1, device_id=(lax.rem(b + d, B), u), device_id_type=MESH
        )

    def send(j, c, side):
        where = rows_buf.at[j, pl.ds(c * part, part), :]
        return pltpu.make_async_remote_copy(
            src_ref=where,
            dst_ref=where,
            send_sem=send_sem.at[side, j, c],
            recv_sem=recv_sem.at[j, c],
            device_id=(b, u - 1 if side == 0 else u + 1),
            device_id_type=MESH,
        )

    def send_if(j, c):
        @pl.when((j >= u) & (u > 0))
        def _():
            send(j, c, 0).start()

        @pl.when((j <= u) & (u < H - 1))
        def _():
            send(j, c, 1).start()

    def normalize(c):
        values = x_ref[pl.ds(c * part, part), :].astype(jnp.float32)
        power = jnp.mean(values * values, axis=1, keepdims=True)
        normed = values * lax.rsqrt(power + eps_norm) * gain_ref[...]
        rows_buf[u, pl.ds(c * part, part), :] = normed.astype(jnp.bfloat16)

    normalize(0)

    @pl.when((u > 0) & (u < H - 1))
    def _():
        pl.semaphore_wait(barrier, B + 1)

    @pl.when((u == 0) | (u == H - 1))
    def _():
        pl.semaphore_wait(barrier, B)

    send_if(u, 0)
    for c in range(1, C):
        normalize(c)
        send_if(u, c)

    starts = segment_starts(seg_ref, segments)
    for copy in weight_copies():
        copy.wait()

    def kv_copy(j, d):
        return pltpu.make_async_remote_copy(
            src_ref=kv_buf.at[j],
            dst_ref=kv_ref.at[pl.ds(pl.multiple_of((b * H + j) * rows, rows), rows), :],
            send_sem=kv_send.at[d, j],
            recv_sem=kv_recv.at[d, j],
            device_id=(b + d, u),
            device_id_type=MESH,
        )

    def kv_own(j):
        return pltpu.make_async_copy(
            kv_buf.at[j],
            kv_ref.at[pl.ds(pl.multiple_of((b * H + j) * rows, rows), rows), :],
            kv_local.at[j],
        )

    def project(j):
        shard = rows_buf[j]
        mask = tenant_mask(starts, adapter_ref, (b * H + j) * rows, rows, HIDDEN)

        def lowered(which):
            raw = jnp.dot(
                shard,
                down_ref[:, which * HIDDEN : (which + 1) * HIDDEN],
                preferred_element_type=jnp.float32,
            )
            return jnp.where(mask, raw, 0.0).astype(jnp.bfloat16)

        def product(column, width, low, up):
            return (
                jnp.dot(
                    shard, weights[:, pl.ds(column, width)], preferred_element_type=jnp.float32
                )
                + adapter_scale * jnp.dot(low, up, preferred_element_type=jnp.float32)
            ).astype(jnp.bfloat16)

        kv_buf[j, :, :kw] = product(0, kw, lowered(1), uk_ref[...])
        kv_buf[j, :, kw:] = product(kw, kw, lowered(2), uv_ref[...])
        kv_own(j).start()
        for d in range(1, B):
            @pl.when(b + d < B)
            def _():
                kv_copy(j, d).start()

        low = lowered(0)
        step = 256

        def query_tile(n, carry):
            at = pl.multiple_of(n * step, step)
            q_ref[pl.ds(pl.multiple_of(j * rows, rows), rows), pl.ds(at, step)] = product(
                2 * kw + at, step, low, uq_ref[:, pl.ds(at, step)]
            )
            return carry

        lax.fori_loop(0, qw // step, query_tile, 0)

    def phase(d, carry):
        @pl.when(d > 0)
        def _():
            for c in range(C):
                @pl.when(u + d < H)
                def _():
                    send(u + d, c, 0).wait_recv()

                    @pl.when(u > 0)
                    def _():
                        send(u + d, c, 0).start()

                @pl.when(u - d >= 0)
                def _():
                    send(u - d, c, 1).wait_recv()

                    @pl.when(u < H - 1)
                    def _():
                        send(u - d, c, 1).start()

        def side_step(side, inner):
            j = u + d * (1 - 2 * side)

            @pl.when((j >= 0) & (j < H) & (d + 1 > side))
            def _():
                project(j)

            return inner

        lax.fori_loop(0, jnp.where(d > 0, 2, 1), side_step, 0)
        return carry

    lax.fori_loop(0, H, phase, 0)

    def finish(j, carry):
        for c in range(C):
            @pl.when((j >= u) & (u > 0))
            def _():
                send(j, c, 0).wait_send()

            @pl.when((j <= u) & (u < H - 1))
            def _():
                send(j, c, 1).wait_send()

        kv_own(j).wait()
        for d in range(1, B):
            @pl.when(b + d < B)
            def _():
                kv_copy(j, d).wait_send()

            @pl.when(b - d >= 0)
            def _():
                kv_copy(j, d).wait_recv()

        return carry

    lax.fori_loop(0, H, finish, 0)


def attention_kernel(
    tile, groups, segments, q_ref, kv_ref, seg_ref, mixed_ref, bias, peak, total
):
    b = lax.axis_index("blk")
    rows = q_ref.shape[0]
    blocks = rows // tile
    group = QUERY_HEADS // KEY_VALUE_HEADS
    scale = math.log2(math.e) / math.sqrt(HEAD_SIZE)
    starts = segment_starts(seg_ref, segments)

    def query_block(qi, carry):
        own = b * blocks + qi
        at_rows = pl.ds(pl.multiple_of(qi * tile, tile), tile)
        pos = (own * tile + lax.broadcasted_iota(jnp.int32, (tile, 1), 0)).astype(jnp.float32)
        lower = jnp.zeros((tile, 1), jnp.float32)
        for k in range(1, segments):
            lower = jnp.where(pos >= starts[k], starts[k], lower)
        first = jnp.min(lower).astype(jnp.int32) // tile
        peak[...] = jnp.full_like(peak, MASKED)
        total[...] = jnp.zeros_like(total)

        def key_tile(i, inner):
            index = own - i
            at_keys = pl.ds(pl.multiple_of(index * tile, tile), tile)
            key_pos = (index * tile + lax.broadcasted_iota(jnp.int32, (tile, tile), 1)).astype(
                jnp.float32
            )
            bias[...] = jnp.where((key_pos <= pos) & (key_pos >= lower), 0.0, MASKED)
            for g in range(groups):
                keys = kv_ref[at_keys, g * HEAD_SIZE : (g + 1) * HEAD_SIZE]
                values = kv_ref[at_keys, (groups + g) * HEAD_SIZE : (groups + g + 1) * HEAD_SIZE]
                values = jnp.concatenate([values, jnp.ones_like(values)], axis=1)
                for h in range(g * group, (g + 1) * group):
                    query = q_ref[at_rows, h * HEAD_SIZE : (h + 1) * HEAD_SIZE]
                    scores = lax.dot_general(
                        query, keys, (((1,), (1,)), ((), ())), preferred_element_type=jnp.float32
                    )
                    scores = scores * scale + bias[...]
                    before = peak[h]
                    fresh = jnp.maximum(before, jnp.max(scores, axis=1, keepdims=True))
                    weights = jnp.exp2(scores - fresh[:, :1]).astype(jnp.bfloat16)
                    decay = jnp.exp2(before - fresh)
                    peak[h] = fresh
                    total[h] = total[h] * jnp.concatenate([decay, decay], axis=1) + jnp.dot(
                        weights, values, preferred_element_type=jnp.float32
                    )
            return inner

        lax.fori_loop(0, own - first + 1, key_tile, 0)
        for h in range(groups * group):
            mixed_ref[at_rows, h * HEAD_SIZE : (h + 1) * HEAD_SIZE] = (
                total[h, :, :HEAD_SIZE] / total[h, :, HEAD_SIZE:]
            ).astype(jnp.bfloat16)
        return carry

    lax.fori_loop(0, blocks, query_block, 0)


def output_kernel(
    H, C, segments,
    mixed_ref, wo_ref, down_ref, up_ref, seg_ref, adapter_ref,
    out_ref,
    left, weights, sent, landed, w_sem, up_sem, send_sem, recv_sem,
):
    u = lax.axis_index("uly")
    b = lax.axis_index("blk")
    rows = out_ref.shape[0]
    inner = mixed_ref.shape[1]
    width = out_ref.shape[1] // C

    def weight_copy(c):
        columns = pl.ds(pl.multiple_of(c * width, width), width)
        return pltpu.make_async_copy(
            wo_ref.at[:, columns], weights.at[pl.ds(0, inner), columns], w_sem.at[c]
        )

    def up_copy(i):
        return pltpu.make_async_copy(
            up_ref, weights.at[pl.ds(inner + i * HIDDEN, HIDDEN), :], up_sem.at[i]
        )

    up_copy(0).start()
    up_copy(1).start()
    for c in range(C):
        weight_copy(c).start()

    barrier = pltpu.get_barrier_semaphore()

    @pl.when(u > 0)
    def _():
        pl.semaphore_signal(barrier, inc=1, device_id=(b, u - 1), device_id_type=MESH)

    @pl.when(u < H - 1)
    def _():
        pl.semaphore_signal(barrier, inc=1, device_id=(b, u + 1), device_id_type=MESH)

    starts = segment_starts(seg_ref, segments)
    total_rows = H * rows
    lows = jnp.dot(mixed_ref[...], down_ref[...], preferred_element_type=jnp.float32)
    mask = tenant_mask(starts, adapter_ref, b * total_rows, total_rows, HIDDEN)
    lows = jnp.where(mask, adapter_scale * lows, 0.0)
    high = lows.astype(jnp.bfloat16)
    left[:, :inner] = mixed_ref[...]
    left[:, inner : inner + HIDDEN] = high
    left[:, inner + HIDDEN :] = (lows - high.astype(jnp.float32)).astype(jnp.bfloat16)

    @pl.when((u > 0) & (u < H - 1))
    def _():
        pl.semaphore_wait(barrier, 2)

    @pl.when((u == 0) | (u == H - 1))
    def _():
        pl.semaphore_wait(barrier, 1)

    up_copy(0).wait()
    up_copy(1).wait()

    def own_part(j, c):
        at_rows = pl.ds(pl.multiple_of(j * rows, rows), rows)
        columns = pl.ds(pl.multiple_of(c * width, width), width)
        return jnp.dot(left[at_rows, :], weights[:, columns], preferred_element_type=jnp.float32)

    def hop(j, c, side):
        return pltpu.make_async_remote_copy(
            src_ref=sent.at[j, c],
            dst_ref=landed.at[side, j, c],
            send_sem=send_sem.at[j, c],
            recv_sem=recv_sem.at[side, j, c],
            device_id=(b, u + 2 * side - 1),
            device_id_type=MESH,
        )

    def step(p, carry):
        def chunk(c, inner_carry):
            @pl.when(p == 0)
            def _():
                weight_copy(c).wait()

            def pass_on(side, side_carry):
                j = jnp.where(side == 0, p, H - 1 - p)

                @pl.when(jnp.where(side == 0, u - j, j - u) > 0)
                def _():
                    value = own_part(j, c)

                    @pl.when(jnp.where(side == 0, H - 1 - u, u) > 0)
                    def _():
                        hop(j, c, side).wait_recv()
                        sent[j, c] = (value + landed[side, j, c].astype(jnp.float32)).astype(
                            jnp.bfloat16
                        )

                    @pl.when(jnp.where(side == 0, H - 1 - u, u) == 0)
                    def _():
                        sent[j, c] = value.astype(jnp.bfloat16)

                    hop(j, c, side).start()

                return side_carry

            lax.fori_loop(0, 2, pass_on, 0)
            return inner_carry

        lax.fori_loop(0, C, chunk, 0)
        return carry

    lax.fori_loop(0, H - 1, step, 0)

    def last(c, carry):
        columns = pl.ds(pl.multiple_of(c * width, width), width)
        sent_own = own_part(u, c)

        @pl.when(u > 0)
        def _():
            hop(u, c, 1).wait_recv()

        @pl.when(u < H - 1)
        def _():
            hop(u, c, 0).wait_recv()

        from_left = jnp.where(u > 0, landed[1, u, c].astype(jnp.float32), 0.0)
        from_right = jnp.where(u < H - 1, landed[0, u, c].astype(jnp.float32), 0.0)
        out_ref[:, columns] = (sent_own + from_left + from_right).astype(jnp.bfloat16)
        return carry

    lax.fori_loop(0, C, last, 0)

    def finish(j, carry):
        for c in range(C):
            @pl.when(j < u)
            def _():
                hop(j, c, 0).wait_send()

            @pl.when(j > u)
            def _():
                hop(j, c, 1).wait_send()

        return carry

    lax.fori_loop(0, H, finish, 0)


IN_VMEM = pl.BlockSpec(memory_space=pltpu.VMEM)
IN_SMEM = pl.BlockSpec(memory_space=pltpu.SMEM)
ANYWHERE = pl.BlockSpec(memory_space=pl.ANY)


def shards(
    activations,
    input_norm_gain,
    query_weight,
    key_weight,
    value_weight,
    output_weight,
    adapter_down_maps,
    query_up_maps,
    key_up_maps,
    value_up_maps,
    output_down_maps,
    output_up_maps,
    segment_index,
    segment_adapter,
):
    H = lax.axis_size("uly")
    B = lax.axis_size("blk")
    rows, features = activations.shape
    tokens = segment_index.shape[0]
    segments = segment_adapter.shape[0]
    qw = query_weight.shape[1]
    kw = key_weight.shape[1]
    block_rows = rows * H
    seg = segment_index.reshape(tokens // 128, 128)
    bf16 = jnp.bfloat16
    C = 3
    queries, keys_values = pl.pallas_call(
        functools.partial(gather_kernel, H, B, C, segments),
        out_shape=(
            jax.ShapeDtypeStruct((block_rows, qw), bf16),
            jax.ShapeDtypeStruct((tokens, 2 * kw), bf16),
        ),
        in_specs=[IN_VMEM, IN_VMEM, IN_VMEM, ANYWHERE, ANYWHERE, ANYWHERE]
        + [IN_VMEM] * 4
        + [IN_SMEM],
        out_specs=(IN_VMEM, ANYWHERE),
        scratch_shapes=[
            pltpu.VMEM((H, rows, features), bf16),
            pltpu.VMEM((features, qw + 2 * kw), bf16),
            pltpu.VMEM((H, rows, 2 * kw), bf16),
            pltpu.SemaphoreType.DMA((3,)),
            pltpu.SemaphoreType.DMA((2, H, C)),
            pltpu.SemaphoreType.DMA((H, C)),
            pltpu.SemaphoreType.DMA((B, H)),
            pltpu.SemaphoreType.DMA((B, H)),
            pltpu.SemaphoreType.DMA((H,)),
        ],
        compiler_params=pltpu.CompilerParams(
            collective_id=0, has_side_effects=True, vmem_limit_bytes=VMEM_LIMIT
        ),
        name="gather_project",
    )(
        activations,
        input_norm_gain.reshape(1, features),
        adapter_down_maps,
        query_weight,
        key_weight,
        value_weight,
        query_up_maps,
        key_up_maps,
        value_up_maps,
        seg,
        segment_adapter,
    )

    tile = math.gcd(block_rows, 384)
    heads = qw // HEAD_SIZE
    mixed = pl.pallas_call(
        functools.partial(attention_kernel, tile, kw // HEAD_SIZE, segments),
        out_shape=jax.ShapeDtypeStruct((block_rows, qw), bf16),
        in_specs=[IN_VMEM] * 3,
        out_specs=IN_VMEM,
        scratch_shapes=[
            pltpu.VMEM((tile, tile), jnp.float32),
            pltpu.VMEM((heads, tile, HEAD_SIZE), jnp.float32),
            pltpu.VMEM((heads, tile, 2 * HEAD_SIZE), jnp.float32),
        ],
        compiler_params=pltpu.CompilerParams(vmem_limit_bytes=VMEM_LIMIT),
        name="attend",
    )(queries, keys_values, seg)

    C = 4
    return pl.pallas_call(
        functools.partial(output_kernel, H, C, segments),
        out_shape=jax.ShapeDtypeStruct((rows, features), bf16),
        in_specs=[IN_VMEM, ANYWHERE, IN_VMEM, ANYWHERE, IN_VMEM, IN_SMEM],
        out_specs=IN_VMEM,
        scratch_shapes=[
            pltpu.VMEM((block_rows, qw + 2 * HIDDEN), bf16),
            pltpu.VMEM((qw + 2 * HIDDEN, features), bf16),
            pltpu.VMEM((H, C, rows, features // C), bf16),
            pltpu.VMEM((2, H, C, rows, features // C), bf16),
            pltpu.SemaphoreType.DMA((C,)),
            pltpu.SemaphoreType.DMA((2,)),
            pltpu.SemaphoreType.DMA((H, C)),
            pltpu.SemaphoreType.DMA((2, H, C)),
        ],
        compiler_params=pltpu.CompilerParams(
            collective_id=1, has_side_effects=True, vmem_limit_bytes=VMEM_LIMIT
        ),
        name="project_reduce",
    )(mixed, output_weight, output_down_maps, output_up_maps, seg, segment_adapter)


def solution(mesh):
    return jax.shard_map(
        shards,
        mesh=mesh,
        in_specs=(
            P(("blk", "uly"), None),
            P(),
            P(None, "uly"),
            P(None, "uly"),
            P(None, "uly"),
            P("uly", None),
            P(),
            P(None, "uly"),
            P(None, "uly"),
            P(None, "uly"),
            P("uly", None),
            P(),
            P(),
            P(),
        ),
        out_specs=P(("blk", "uly"), None),
        check_vma=False,
    )
```

time: 283 us -> 168 us (0.59); the launches traced: 280 us -> 168 us
  Pallas kernels: 0 us -> 166 us
  waiting for transfers between devices: 158 us -> 0 us
  matrix products: 56.4 us -> 0 us
  local copies, waits for them, and re-layouts: 29 us -> 2.06 us
  other arithmetic: 19.1 us -> 0 us
  between operations: 13.3 us -> 0.02 us
  loops' own time: 4.12 us -> 0 us
    pallas_call x0 -> x3, Pallas kernels: none -> 166 us  [the longest x1 86.7 us: shards(): pl.pallas_call(functools.partial(output_kernel, H, C, segments), out_shap...]
    all_gather x3 -> x0, waiting for transfers between devices: 95.9 us -> none  [the longest x1 67.1 us: shards(): piece = lax.all_gather(packed, 'uly', axis=0, tiled=True)]
    reduce_scatter x1 -> x0, waiting for transfers between devices: 62 us -> none  [shards(): lax.psum_scatter(jnp.concatenate([jnp.dot(mixed_heads, output_weight, pre...]
    dot_general x22 -> x0, matrix products: 56.4 us -> none  [the longest x6 14.3 us: compute(): jnp.einsum('rkgd,nkd->rkgn', query_matrix, key_block, preferred_element_t...]
    reduce_sum x9 -> x0, other arithmetic: 10.2 us -> none  [the longest x6 7.81 us: compute(): total = total * decay + jnp.sum(weights, axis=3)]
    dynamic_slice x14 -> x0, local copies, waits for them, and re-layouts: 7.82 us -> none  [the longest x6 6.44 us: compute(): lax.dynamic_slice_in_dim(value_piece, offset, step)]
    cond x30 -> x0, local copies, waits for them, and re-layouts: 7.33 us -> none
    unnamed x19 -> x1, local copies, waits for them, and re-layouts: 7.34 us -> 2.06 us
  transfers between devices with their start and end apart: 4 -> 0, of which waited for: 4 -> 0; matrix products, arithmetic and copies ran while one was open for 9% -> 0% of each run, Pallas kernels for 0% -> 0%
where the time goes in v1:
time: 168 us
  Pallas kernels  166 us (99%)
  local copies, waits for them, and re-layouts  2.06 us (1%)
    pallas_call x1, Pallas kernels, shards(): pl.pallas_call(functools.partial(output_kernel, H, C, segments), out_shap...  86.7 us
    pallas_call x1, Pallas kernels, shards(): pl.pallas_call(functools.partial(gather_kernel, H, B, C, segments), out_s...  55.4 us
    pallas_call x1, Pallas kernels, shards(): pl.pallas_call(functools.partial(attention_kernel, tile, kw // HEAD_SIZE,...  24 us

profile of v1, /device:TPU:15, one launch (start us, length us, event | category | flops | bytes accessed | tf_op | source)
XLA Modules:
  0.0 168.1 jit_solution(12462376286739297643)
XLA Ops:
  0.0 55.4 %gather_project.1 = (bf16[384,1024]{1,0:T(8,128)(2,1)}, bf16[3072,512]{1,0:T(8,128)(2,1)}) custom-call(bf16[96,4096]{1,0:T(8,128)(2,1)} %x_ref.1, f32[1,4096]{1,0:T(1,128)} %bitcast.5, bf16[4096,384]{1,0:T(8,128)(2,1)} %down_ref.2, bf16[4096,1024]{1,0:T(8,128)(2,1)} %wq_ref.1, bf16[4096,256]{1,0:T(8,128)(2,1)} %wk_ref.1, bf16[4096,256]{1,0:T(8,128)(2,1)} %wv_ref.1, ...), custom_call_target="tpu_custom_call" | custom-call | tf_op jit(solution)/shard_map/gather_project/pallas_call | solution.py:477
  55.4 24.0 %attend.1.mixed_ref = bf16[384,1024]{1,0:T(8,128)(2,1)} custom-call(bf16[384,1024]{1,0:T(8,128)(2,1)} %get-tuple-element.7.q_ref, bf16[3072,512]{1,0:T(8,128)(2,1)} %get-tuple-element.8.kv_ref, s32[24,128]{1,0:T(8,128)} %bitcast.3), custom_call_target="tpu_custom_call" | custom-call | tf_op jit(solution)/shard_map/attend/pallas_call | solution.py:518
  79.4 86.7 %project_reduce.1 = bf16[96,4096]{1,0:T(8,128)(2,1)} custom-call(bf16[384,1024]{1,0:T(8,128)(2,1)} %attend.1.mixed_ref, bf16[1024,4096]{1,0:T(8,128)(2,1)} %wo_ref.1, bf16[1024,128]{1,0:T(8,128)(2,1)} %down_ref.3, bf16[128,4096]{1,0:T(8,128)(2,1)} %up_ref.1, s32[24,128]{1,0:T(8,128)} %bitcast.4, s32[4]{0:T(128)} %adapter_ref.3), custom_call_target="tpu_custom_call" | custom-call | tf_op jit(solution)/shard_map/project_reduce/pallas_call | solution.py:533
  166.1 2.1 %copy.16 = bf16[96,4096]{1,0:T(8,128)(2,1)} copy(bf16[96,4096]{1,0:T(8,128)(2,1)} %project_reduce.1) | data formatting | bytes 1572864

commit v2 on v1

v2 whole, which is shorter than its diff:
```python
import functools
import math

import jax
import jax.numpy as jnp
from jax import lax
from jax.experimental import pallas as pl
from jax.experimental.pallas import tpu as pltpu
from jax.sharding import PartitionSpec as P

QUERY_HEADS = 32
KEY_VALUE_HEADS = 8
HEAD_SIZE = 128
ADAPTER_RANK = 16
ADAPTER_COUNT = 8
HIDDEN = ADAPTER_COUNT * ADAPTER_RANK

eps_norm = 1e-05
adapter_scale = 2.0
MESH = pl.DeviceIdType.MESH
VMEM_LIMIT = 60 * 1024 * 1024
MASKED = -1e30


def segment_starts(seg_ref, segments):
    seg = seg_ref[...]
    starts = []
    for k in range(segments):
        below = jnp.where(seg < k, 1.0, 0.0)
        starts.append(jnp.sum(jnp.sum(below, axis=1, keepdims=True), axis=0, keepdims=True))
    return starts


def tenant_mask(starts, adapter_ref, first, rows, width):
    pos = (first + lax.broadcasted_iota(jnp.int32, (rows, width), 0)).astype(jnp.float32)
    column = lax.broadcasted_iota(jnp.int32, (rows, width), 1)
    column = (column // ADAPTER_RANK) % ADAPTER_COUNT
    tenant = jnp.zeros((rows, width), jnp.int32) + adapter_ref[0]
    for k in range(1, len(starts)):
        tenant = jnp.where(pos >= starts[k], adapter_ref[k], tenant)
    return column == tenant


def block_kernel(
    H, B, C, D, T, segments,
    x_ref, gain_ref, down_ref, wq_ref, wk_ref, wv_ref, uq_ref, uk_ref, uv_ref,
    wo_ref, out_down_ref, out_up_ref, seg_ref, adapter_ref,
    out_ref,
    rows_buf, weights, down, q_buf, kv, peak, total, left, out_weights, sent, landed,
    w_sem, o_sem, send_sem, recv_sem, kv_send, kv_recv, hop_send, hop_recv,
):
    u = lax.axis_index("uly")
    b = lax.axis_index("blk")
    rows, features = x_ref.shape
    part = rows // C
    kw = wk_ref.shape[1]
    qw = wq_ref.shape[1]
    width = features // D

    def weight_copies():
        return [
            pltpu.make_async_copy(down_ref, down, w_sem.at[0]),
            pltpu.make_async_copy(wk_ref, weights.at[:, pl.ds(0, kw)], w_sem.at[1]),
            pltpu.make_async_copy(wv_ref, weights.at[:, pl.ds(kw, kw)], w_sem.at[2]),
            pltpu.make_async_copy(wq_ref, weights.at[:, pl.ds(2 * kw, qw)], w_sem.at[3]),
        ]

    def output_copies():
        return [
            pltpu.make_async_copy(wo_ref, out_weights.at[pl.ds(0, qw), :], o_sem.at[0]),
            pltpu.make_async_copy(
                out_up_ref, out_weights.at[pl.ds(qw, HIDDEN), :], o_sem.at[1]
            ),
            pltpu.make_async_copy(
                out_up_ref, out_weights.at[pl.ds(qw + HIDDEN, HIDDEN), :], o_sem.at[2]
            ),
        ]

    for copy in weight_copies():
        copy.start()
    kv[...] = jnp.zeros_like(kv)

    barrier = pltpu.get_barrier_semaphore()

    @pl.when(u > 0)
    def _():
        pl.semaphore_signal(barrier, inc=1, device_id=(b, u - 1), device_id_type=MESH)

    @pl.when(u < H - 1)
    def _():
        pl.semaphore_signal(barrier, inc=1, device_id=(b, u + 1), device_id_type=MESH)

    for d in range(1, B):
        pl.semaphore_signal(
            barrier, inc=1, device_id=(lax.rem(b + d, B), u), device_id_type=MESH
        )

    def send(j, c, side):
        where = rows_buf.at[j, pl.ds(c * part, part), :]
        return pltpu.make_async_remote_copy(
            src_ref=where,
            dst_ref=where,
            send_sem=send_sem.at[side, j, c],
            recv_sem=recv_sem.at[j, c],
            device_id=(b, u - 1 if side == 0 else u + 1),
            device_id_type=MESH,
        )

    def send_if(j, c):
        @pl.when((j >= u) & (u > 0))
        def _():
            send(j, c, 0).start()

        @pl.when((j <= u) & (u < H - 1))
        def _():
            send(j, c, 1).start()

    def normalize(c):
        values = x_ref[pl.ds(c * part, part), :].astype(jnp.float32)
        power = jnp.mean(values * values, axis=1, keepdims=True)
        normed = values * lax.rsqrt(power + eps_norm) * gain_ref[...]
        rows_buf[u, pl.ds(c * part, part), :] = normed.astype(jnp.bfloat16)

    normalize(0)

    @pl.when((u > 0) & (u < H - 1))
    def _():
        pl.semaphore_wait(barrier, B + 1)

    @pl.when((u == 0) | (u == H - 1))
    def _():
        pl.semaphore_wait(barrier, B)

    send_if(u, 0)
    for c in range(1, C):
        normalize(c)
        send_if(u, c)

    starts = segment_starts(seg_ref, segments)
    for copy in weight_copies():
        copy.wait()
    for copy in output_copies():
        copy.start()

    def shard_rows(block, j):
        return pl.ds(pl.multiple_of((block * H + j) * rows, rows), rows)

    def kv_copy(j, d):
        where = kv.at[shard_rows(b, j), :]
        return pltpu.make_async_remote_copy(
            src_ref=where,
            dst_ref=where,
            send_sem=kv_send.at[d, j],
            recv_sem=kv_recv.at[d, j],
            device_id=(b + d, u),
            device_id_type=MESH,
        )

    def project(j):
        shard = rows_buf[j]
        mask = tenant_mask(starts, adapter_ref, (b * H + j) * rows, rows, HIDDEN)

        def lowered(which):
            raw = jnp.dot(
                shard,
                down[:, which * HIDDEN : (which + 1) * HIDDEN],
                preferred_element_type=jnp.float32,
            )
            return jnp.where(mask, raw, 0.0).astype(jnp.bfloat16)

        def product(column, width, low, up):
            return (
                jnp.dot(
                    shard, weights[:, pl.ds(column, width)], preferred_element_type=jnp.float32
                )
                + adapter_scale * jnp.dot(low, up, preferred_element_type=jnp.float32)
            ).astype(jnp.bfloat16)

        kv[shard_rows(b, j), :kw] = product(0, kw, lowered(1), uk_ref[...])
        kv[shard_rows(b, j), kw:] = product(kw, kw, lowered(2), uv_ref[...])
        for d in range(1, B):
            @pl.when(b + d < B)
            def _():
                kv_copy(j, d).start()

        low = lowered(0)
        step = 256

        def query_tile(n, carry):
            at = pl.multiple_of(n * step, step)
            q_buf[shard_rows(0, j), pl.ds(at, step)] = product(
                2 * kw + at, step, low, uq_ref[:, pl.ds(at, step)]
            )
            return carry

        lax.fori_loop(0, qw // step, query_tile, 0)

    def phase(d, carry):
        @pl.when(d > 0)
        def _():
            for c in range(C):
                @pl.when(u + d < H)
                def _():
                    send(u + d, c, 0).wait_recv()

                    @pl.when(u > 0)
                    def _():
                        send(u + d, c, 0).start()

                @pl.when(u - d >= 0)
                def _():
                    send(u - d, c, 1).wait_recv()

                    @pl.when(u < H - 1)
                    def _():
                        send(u - d, c, 1).start()

        def side_step(side, inner):
            j = u + d * (1 - 2 * side)

            @pl.when((j >= 0) & (j < H) & (d + 1 > side))
            def _():
                project(j)

            return inner

        lax.fori_loop(0, jnp.where(d > 0, 2, 1), side_step, 0)
        return carry

    lax.fori_loop(0, H, phase, 0)

    def keys_arrived(j, carry):
        for d in range(1, B):
            @pl.when(b - d >= 0)
            def _():
                kv_copy(j, d).wait_recv()

        return carry

    lax.fori_loop(0, H, keys_arrived, 0)

    groups = kw // HEAD_SIZE
    group = QUERY_HEADS // KEY_VALUE_HEADS
    scale = math.log2(math.e) / math.sqrt(HEAD_SIZE)

    def attend(j):
        at_rows = shard_rows(0, j)
        first = (b * H + j) * rows
        pos = (first + lax.broadcasted_iota(jnp.int32, (rows, 1), 0)).astype(jnp.float32)
        lower = jnp.zeros((rows, 1), jnp.float32)
        for k in range(1, segments):
            lower = jnp.where(pos >= starts[k], starts[k], lower)
        peak[...] = jnp.full_like(peak, MASKED)
        total[...] = jnp.zeros_like(total)
        tiles = (first + rows - 1) // T + 1

        def key_tile(i, inner):
            index = tiles - 1 - i
            at_keys = pl.ds(pl.multiple_of(index * T, T), T)
            key_pos = (index * T + lax.broadcasted_iota(jnp.int32, (rows, T), 1)).astype(
                jnp.float32
            )
            bias = jnp.where((key_pos <= pos) & (key_pos >= lower), 0.0, MASKED)
            bias = jnp.concatenate([bias] * group, axis=0)
            for g in range(groups):
                keys = kv[at_keys, g * HEAD_SIZE : (g + 1) * HEAD_SIZE]
                values = kv[at_keys, (groups + g) * HEAD_SIZE : (groups + g + 1) * HEAD_SIZE]
                values = jnp.concatenate([values, jnp.ones_like(values)], axis=1)
                query = jnp.concatenate(
                    [
                        q_buf[at_rows, h * HEAD_SIZE : (h + 1) * HEAD_SIZE]
                        for h in range(g * group, (g + 1) * group)
                    ],
                    axis=0,
                )
                scores = lax.dot_general(
                    query, keys, (((1,), (1,)), ((), ())), preferred_element_type=jnp.float32
                )
                scores = scores * scale + bias
                before = peak[g]
                fresh = jnp.maximum(before, jnp.max(scores, axis=1, keepdims=True))
                shares = jnp.exp2(scores - fresh[:, :1]).astype(jnp.bfloat16)
                decay = jnp.exp2(before - fresh)
                peak[g] = fresh
                total[g] = total[g] * jnp.concatenate([decay, decay], axis=1) + jnp.dot(
                    shares, values, preferred_element_type=jnp.float32
                )
            return inner

        lax.fori_loop(0, tiles, key_tile, 0)
        for h in range(groups * group):
            g, at = h // group, (h % group) * rows
            left[at_rows, h * HEAD_SIZE : (h + 1) * HEAD_SIZE] = (
                total[g, at : at + rows, :HEAD_SIZE] / total[g, at : at + rows, HEAD_SIZE:]
            ).astype(jnp.bfloat16)
        lows = jnp.dot(
            left[at_rows, :qw], out_down_ref[...], preferred_element_type=jnp.float32
        )
        mask = tenant_mask(starts, adapter_ref, first, rows, HIDDEN)
        lows = jnp.where(mask, adapter_scale * lows, 0.0)
        high = lows.astype(jnp.bfloat16)
        left[at_rows, qw : qw + HIDDEN] = high
        left[at_rows, qw + HIDDEN :] = (lows - high.astype(jnp.float32)).astype(jnp.bfloat16)

    def own_part(j, c):
        columns = pl.ds(pl.multiple_of(c * width, width), width)
        return jnp.dot(
            left[shard_rows(0, j), :], out_weights[:, columns], preferred_element_type=jnp.float32
        )

    def hop(j, c, side):
        return pltpu.make_async_remote_copy(
            src_ref=sent.at[j, c],
            dst_ref=landed.at[side, j, c],
            send_sem=hop_send.at[j, c],
            recv_sem=hop_recv.at[side, j, c],
            device_id=(b, u + 2 * side - 1),
            device_id_type=MESH,
        )

    for copy in output_copies():
        copy.wait()

    def step(p, carry):
        def side_shard(side):
            j = jnp.where(side == 0, p, H - 1 - p)
            return j, jnp.where(side == 0, u - j, j - u) > 0

        def attend_any(side, side_carry):
            j, further = side_shard(side)
            final = p == H - 1

            @pl.when((final & (side == 0)) | ((p < H - 1) & further))
            def _():
                attend(jnp.where(final, u, j))

            return side_carry

        lax.fori_loop(0, 2, attend_any, 0)

        def chunk(c, inner_carry):
            def pass_on(side, side_carry):
                j, further = side_shard(side)
                behind = jnp.where(side == 0, H - 1 - u, u)

                @pl.when(further)
                def _():
                    value = own_part(j, c)

                    @pl.when(behind > 0)
                    def _():
                        hop(j, c, side).wait_recv()
                        sent[j, c] = (value + landed[side, j, c].astype(jnp.float32)).astype(
                            jnp.bfloat16
                        )

                    @pl.when(behind == 0)
                    def _():
                        sent[j, c] = value.astype(jnp.bfloat16)

                    hop(j, c, side).start()

                return side_carry

            lax.fori_loop(0, 2, pass_on, 0)
            return inner_carry

        @pl.when(p < H - 1)
        def _():
            lax.fori_loop(0, D, chunk, 0)

        return carry

    lax.fori_loop(0, H, step, 0)

    def last(c, carry):
        columns = pl.ds(pl.multiple_of(c * width, width), width)
        value = own_part(u, c)

        @pl.when(u > 0)
        def _():
            hop(u, c, 1).wait_recv()

        @pl.when(u < H - 1)
        def _():
            hop(u, c, 0).wait_recv()

        from_left = jnp.where(u > 0, landed[1, u, c].astype(jnp.float32), 0.0)
        from_right = jnp.where(u < H - 1, landed[0, u, c].astype(jnp.float32), 0.0)
        out_ref[:, columns] = (value + from_left + from_right).astype(jnp.bfloat16)
        return carry

    lax.fori_loop(0, D, last, 0)

    def finish(j, carry):
        for c in range(C):
            @pl.when((j >= u) & (u > 0))
            def _():
                send(j, c, 0).wait_send()

            @pl.when((j <= u) & (u < H - 1))
            def _():
                send(j, c, 1).wait_send()

        for d in range(1, B):
            @pl.when(b + d < B)
            def _():
                kv_copy(j, d).wait_send()

        for c in range(D):
            @pl.when(j != u)
            def _():
                hop(j, c, jnp.where(j < u, 0, 1)).wait_send()

        return carry

    lax.fori_loop(0, H, finish, 0)


IN_VMEM = pl.BlockSpec(memory_space=pltpu.VMEM)
IN_SMEM = pl.BlockSpec(memory_space=pltpu.SMEM)
ANYWHERE = pl.BlockSpec(memory_space=pl.ANY)


def shards(
    activations,
    input_norm_gain,
    query_weight,
    key_weight,
    value_weight,
    output_weight,
    adapter_down_maps,
    query_up_maps,
    key_up_maps,
    value_up_maps,
    output_down_maps,
    output_up_maps,
    segment_index,
    segment_adapter,
):
    H = lax.axis_size("uly")
    B = lax.axis_size("blk")
    rows, features = activations.shape
    tokens = segment_index.shape[0]
    segments = segment_adapter.shape[0]
    qw = query_weight.shape[1]
    kw = key_weight.shape[1]
    block_rows = rows * H
    seg = segment_index.reshape(tokens // 128, 128)
    bf16 = jnp.bfloat16
    C, D = 3, 4
    T = math.gcd(tokens, 512)
    group_rows = QUERY_HEADS // KEY_VALUE_HEADS * rows
    groups = kw // HEAD_SIZE
    f32 = jnp.float32
    return pl.pallas_call(
        functools.partial(block_kernel, H, B, C, D, T, segments),
        out_shape=jax.ShapeDtypeStruct((rows, features), bf16),
        in_specs=[IN_VMEM] * 2
        + [ANYWHERE] * 4
        + [IN_VMEM] * 3
        + [ANYWHERE, IN_VMEM, ANYWHERE, IN_VMEM, IN_SMEM],
        out_specs=IN_VMEM,
        scratch_shapes=[
            pltpu.VMEM((H, rows, features), bf16),
            pltpu.VMEM((features, qw + 2 * kw), bf16),
            pltpu.VMEM(adapter_down_maps.shape, bf16),
            pltpu.VMEM((block_rows, qw), bf16),
            pltpu.VMEM((tokens, 2 * kw), bf16),
            pltpu.VMEM((groups, group_rows, HEAD_SIZE), f32),
            pltpu.VMEM((groups, group_rows, 2 * HEAD_SIZE), f32),
            pltpu.VMEM((block_rows, qw + 2 * HIDDEN), bf16),
            pltpu.VMEM((qw + 2 * HIDDEN, features), bf16),
            pltpu.VMEM((H, D, rows, features // D), bf16),
            pltpu.VMEM((2, H, D, rows, features // D), bf16),
            pltpu.SemaphoreType.DMA((4,)),
            pltpu.SemaphoreType.DMA((3,)),
            pltpu.SemaphoreType.DMA((2, H, C)),
            pltpu.SemaphoreType.DMA((H, C)),
            pltpu.SemaphoreType.DMA((B, H)),
            pltpu.SemaphoreType.DMA((B, H)),
            pltpu.SemaphoreType.DMA((H, D)),
            pltpu.SemaphoreType.DMA((2, H, D)),
        ],
        compiler_params=pltpu.CompilerParams(
            collective_id=0, has_side_effects=True, vmem_limit_bytes=VMEM_LIMIT
        ),
        name="attention_block",
    )(
        activations,
        input_norm_gain.reshape(1, features),
        adapter_down_maps,
        query_weight,
        key_weight,
        value_weight,
        query_up_maps,
        key_up_maps,
        value_up_maps,
        output_weight,
        output_down_maps,
        output_up_maps,
        seg,
        segment_adapter,
    )


def solution(mesh):
    return jax.shard_map(
        shards,
        mesh=mesh,
        in_specs=(
            P(("blk", "uly"), None),
            P(),
            P(None, "uly"),
            P(None, "uly"),
            P(None, "uly"),
            P("uly", None),
            P(),
            P(None, "uly"),
            P(None, "uly"),
            P(None, "uly"),
            P("uly", None),
            P(),
            P(),
            P(),
        ),
        out_specs=P(("blk", "uly"), None),
        check_vma=False,
    )
```

time: 168 us -> 160 us (0.952)
  Pallas kernels: 166 us -> 157 us
    pallas_call x3 -> x1, Pallas kernels: 166 us -> 157 us  [shards(): pl.pallas_call(functools.partial(block_kernel, H, B, C, D, T, segments),...]
where the time goes in v2:
time: 160 us; the launch traced here: 159 us
  Pallas kernels  157 us (98%)
  local copies, waits for them, and re-layouts  2.06 us (1%)
    pallas_call x1, Pallas kernels, shards(): pl.pallas_call(functools.partial(block_kernel, H, B, C, D, T, segments),...  157 us

profile of v2, /device:TPU:15, one launch (start us, length us, event | category | flops | bytes accessed | tf_op | source)
XLA Modules:
  0.0 159.1 jit_solution(6550882551721122982)
XLA Ops:
  0.0 157.0 %attention_block.1 = bf16[96,4096]{1,0:T(8,128)(2,1)} custom-call(bf16[96,4096]{1,0:T(8,128)(2,1)} %x_ref.1, f32[1,4096]{1,0:T(1,128)} %bitcast.2, bf16[4096,384]{1,0:T(8,128)(2,1)} %down_ref.1, bf16[4096,1024]{1,0:T(8,128)(2,1)} %wq_ref.1, bf16[4096,256]{1,0:T(8,128)(2,1)} %wk_ref.1, bf16[4096,256]{1,0:T(8,128)(2,1)} %wv_ref.1, bf16[128,1024]{1,0:T(8,128)(2,1)} %uq_ref.1, ...), custom_call_target="tpu_custom_call" | custom-call | tf_op jit(solution)/shard_map/attention_block/pallas_call | solution.py:456
  157.0 2.1 %copy.16 = bf16[96,4096]{1,0:T(8,128)(2,1)} copy(bf16[96,4096]{1,0:T(8,128)(2,1)} %attention_block.1) | data formatting | bytes 1572864

commit v3 on v2

--- a/solution.py
+++ b/solution.py
@@ -20,6 +20,7 @@
 MESH = pl.DeviceIdType.MESH
 VMEM_LIMIT = 60 * 1024 * 1024
 MASKED = -1e30
+LAG = 2
 
 
 def segment_starts(seg_ref, segments):
@@ -261,7 +262,6 @@
                 jnp.float32
             )
             bias = jnp.where((key_pos <= pos) & (key_pos >= lower), 0.0, MASKED)
-            bias = jnp.concatenate([bias] * group, axis=0)
             for g in range(groups):
                 keys = kv[at_keys, g * HEAD_SIZE : (g + 1) * HEAD_SIZE]
                 values = kv[at_keys, (groups + g) * HEAD_SIZE : (groups + g + 1) * HEAD_SIZE]
@@ -276,7 +276,8 @@
                 scores = lax.dot_general(
                     query, keys, (((1,), (1,)), ((), ())), preferred_element_type=jnp.float32
                 )
-                scores = scores * scale + bias
+                scores = scores.reshape(group, rows, T) * scale + bias[None]
+                scores = scores.reshape(group * rows, T)
                 before = peak[g]
                 fresh = jnp.maximum(before, jnp.max(scores, axis=1, keepdims=True))
                 shares = jnp.exp2(scores - fresh[:, :1]).astype(jnp.bfloat16)
@@ -321,57 +322,61 @@
     for copy in output_copies():
         copy.wait()
 
-    def step(p, carry):
-        def side_shard(side):
-            j = jnp.where(side == 0, p, H - 1 - p)
-            return j, jnp.where(side == 0, u - j, j - u) > 0
-
-        def attend_any(side, side_carry):
-            j, further = side_shard(side)
-            final = p == H - 1
-
-            @pl.when((final & (side == 0)) | ((p < H - 1) & further))
-            def _():
-                attend(jnp.where(final, u, j))
+    hops = (H - 1) * D
+    final = 1 + hops + LAG * (H - 2)
+
+    def place(n, side):
+        p = n // D
+        j = jnp.where(side == 0, p, H - 1 - p)
+        sends = jnp.where(side == 0, u - j, j - u) > 0
+        return j, n % D, sends
+
+    def step(t, carry):
+        def position(side):
+            behind = jnp.where(side == 0, H - 1 - u, u)
+            n = t - 1 - LAG * jnp.maximum(behind - 1, 0)
+            return jnp.clip(n, 0, hops - 1), (n >= 0) & (n < hops), behind
+
+        def attend_side(side, side_carry):
+            n, inside, _ = position(side)
+            j, c, sends = place(jnp.where(t == 0, 0, n), side)
+            due = (t == 0) | (inside & (c == 0) & (n > 0))
+
+            @pl.when(((t < final) & sends & due) | ((t == final) & (side == 0)))
+            def _():
+                attend(jnp.where(t == final, u, j))
 
             return side_carry
 
-        lax.fori_loop(0, 2, attend_any, 0)
-
-        def chunk(c, inner_carry):
-            def pass_on(side, side_carry):
-                j, further = side_shard(side)
-                behind = jnp.where(side == 0, H - 1 - u, u)
-
-                @pl.when(further)
+        lax.fori_loop(0, 2, attend_side, 0)
+
+        def pass_on(side, side_carry):
+            n, inside, behind = position(side)
+            j, c, sends = place(n, side)
+
+            @pl.when(inside & sends)
+            def _():
+                value = own_part(j, c)
+
+                @pl.when(behind > 0)
                 def _():
-                    value = own_part(j, c)
-
-                    @pl.when(behind > 0)
-                    def _():
-                        hop(j, c, side).wait_recv()
-                        sent[j, c] = (value + landed[side, j, c].astype(jnp.float32)).astype(
-                            jnp.bfloat16
-                        )
-
-                    @pl.when(behind == 0)
-                    def _():
-                        sent[j, c] = value.astype(jnp.bfloat16)
-
-                    hop(j, c, side).start()
-
-                return side_carry
-
-            lax.fori_loop(0, 2, pass_on, 0)
-            return inner_carry
-
-        @pl.when(p < H - 1)
-        def _():
-            lax.fori_loop(0, D, chunk, 0)
-
+                    hop(j, c, side).wait_recv()
+                    sent[j, c] = (value + landed[side, j, c].astype(jnp.float32)).astype(
+                        jnp.bfloat16
+                    )
+
+                @pl.when(behind == 0)
+                def _():
+                    sent[j, c] = value.astype(jnp.bfloat16)
+
+                hop(j, c, side).start()
+
+            return side_carry
+
+        lax.fori_loop(0, 2, pass_on, 0)
         return carry
 
-    lax.fori_loop(0, H, step, 0)
+    lax.fori_loop(0, final + 1, step, 0)
 
     def last(c, carry):
         columns = pl.ds(pl.multiple_of(c * width, width), width)
@@ -449,7 +454,7 @@
     seg = segment_index.reshape(tokens // 128, 128)
     bf16 = jnp.bfloat16
     C, D = 3, 4
-    T = math.gcd(tokens, 512)
+    T = math.gcd(tokens, 1024)
     group_rows = QUERY_HEADS // KEY_VALUE_HEADS * rows
     groups = kw // HEAD_SIZE
     f32 = jnp.float32

time: 160 us -> 132 us (0.82)
  Pallas kernels: 157 us -> 129 us
    pallas_call x1, Pallas kernels: 157 us -> 129 us  [shards(): pl.pallas_call(functools.partial(block_kernel, H, B, C, D, T, segments),...]
where the time goes in v3:
time: 132 us; the launch traced here: 131 us
  Pallas kernels  129 us (98%)
  local copies, waits for them, and re-layouts  2.06 us (2%)
    pallas_call x1, Pallas kernels, shards(): pl.pallas_call(functools.partial(block_kernel, H, B, C, D, T, segments),...  129 us

profile of v3, /device:TPU:15, one launch (start us, length us, event | category | flops | bytes accessed | tf_op | source)
XLA Modules:
  0.0 131.3 jit_solution(2496808576146119699)
XLA Ops:
  0.0 129.2 %attention_block.1 = bf16[96,4096]{1,0:T(8,128)(2,1)} custom-call(bf16[96,4096]{1,0:T(8,128)(2,1)} %x_ref.1, f32[1,4096]{1,0:T(1,128)} %bitcast.2, bf16[4096,384]{1,0:T(8,128)(2,1)} %down_ref.1, bf16[4096,1024]{1,0:T(8,128)(2,1)} %wq_ref.1, bf16[4096,256]{1,0:T(8,128)(2,1)} %wk_ref.1, bf16[4096,256]{1,0:T(8,128)(2,1)} %wv_ref.1, bf16[128,1024]{1,0:T(8,128)(2,1)} %uq_ref.1, ...), custom_call_target="tpu_custom_call" | custom-call | tf_op jit(solution)/shard_map/attention_block/pallas_call | solution.py:461
  129.2 2.1 %copy.16 = bf16[96,4096]{1,0:T(8,128)(2,1)} copy(bf16[96,4096]{1,0:T(8,128)(2,1)} %attention_block.1) | data formatting | bytes 1572864

commit v4 on v3

--- a/solution.py
+++ b/solution.py
@@ -3,6 +3,7 @@
 
 import jax
 import jax.numpy as jnp
+import numpy as np
 from jax import lax
 from jax.experimental import pallas as pl
 from jax.experimental.pallas import tpu as pltpu
@@ -43,9 +44,9 @@
 
 
 def block_kernel(
-    H, B, C, D, T, segments,
+    H, B, C, D, segments,
     x_ref, gain_ref, down_ref, wq_ref, wk_ref, wv_ref, uq_ref, uk_ref, uv_ref,
-    wo_ref, out_down_ref, out_up_ref, seg_ref, adapter_ref,
+    wo_ref, out_down_ref, out_up_ref, seg_ref, key_pos_ref, adapter_ref,
     out_ref,
     rows_buf, weights, down, q_buf, kv, peak, total, left, out_weights, sent, landed,
     w_sem, o_sem, send_sem, recv_sem, kv_send, kv_recv, hop_send, hop_recv,
@@ -143,11 +144,14 @@
     for copy in output_copies():
         copy.start()
 
-    def shard_rows(block, j):
-        return pl.ds(pl.multiple_of((block * H + j) * rows, rows), rows)
+    def shard_rows(j):
+        return pl.ds(pl.multiple_of(j * rows, rows), rows)
+
+    def key_rows(block, j):
+        return pl.ds(pl.multiple_of((j * B + block) * rows, rows), rows)
 
     def kv_copy(j, d):
-        where = kv.at[shard_rows(b, j), :]
+        where = kv.at[key_rows(b, j), :]
         return pltpu.make_async_remote_copy(
             src_ref=where,
             dst_ref=where,
@@ -177,8 +181,8 @@
                 + adapter_scale * jnp.dot(low, up, preferred_element_type=jnp.float32)
             ).astype(jnp.bfloat16)
 
-        kv[shard_rows(b, j), :kw] = product(0, kw, lowered(1), uk_ref[...])
-        kv[shard_rows(b, j), kw:] = product(kw, kw, lowered(2), uv_ref[...])
+        kv[key_rows(b, j), :kw] = product(0, kw, lowered(1), uk_ref[...])
+        kv[key_rows(b, j), kw:] = product(kw, kw, lowered(2), uv_ref[...])
         for d in range(1, B):
             @pl.when(b + d < B)
             def _():
@@ -189,78 +193,50 @@
 
         def query_tile(n, carry):
             at = pl.multiple_of(n * step, step)
-            q_buf[shard_rows(0, j), pl.ds(at, step)] = product(
+            q_buf[shard_rows(j), pl.ds(at, step)] = product(
                 2 * kw + at, step, low, uq_ref[:, pl.ds(at, step)]
             )
             return carry
 
         lax.fori_loop(0, qw // step, query_tile, 0)
 
-    def phase(d, carry):
-        @pl.when(d > 0)
-        def _():
-            for c in range(C):
-                @pl.when(u + d < H)
+    at_end = (u == 0) | (u == H - 1)
+
+    def await_keys(known):
+        def keys_arrived(j, carry):
+            early = at_end & (j != H - 1 - u)
+            for d in range(1, B):
+                @pl.when((b - d >= 0) & (early if known else jnp.logical_not(early)))
                 def _():
-                    send(u + d, c, 0).wait_recv()
-
-                    @pl.when(u > 0)
-                    def _():
-                        send(u + d, c, 0).start()
-
-                @pl.when(u - d >= 0)
-                def _():
-                    send(u - d, c, 1).wait_recv()
-
-                    @pl.when(u < H - 1)
-                    def _():
-                        send(u - d, c, 1).start()
-
-        def side_step(side, inner):
-            j = u + d * (1 - 2 * side)
-
-            @pl.when((j >= 0) & (j < H) & (d + 1 > side))
-            def _():
-                project(j)
-
-            return inner
-
-        lax.fori_loop(0, jnp.where(d > 0, 2, 1), side_step, 0)
-        return carry
-
-    lax.fori_loop(0, H, phase, 0)
-
-    def keys_arrived(j, carry):
-        for d in range(1, B):
-            @pl.when(b - d >= 0)
-            def _():
-                kv_copy(j, d).wait_recv()
-
-        return carry
-
-    lax.fori_loop(0, H, keys_arrived, 0)
+                    kv_copy(j, d).wait_recv()
+
+            return carry
+
+        lax.fori_loop(0, H, keys_arrived, 0)
 
     groups = kw // HEAD_SIZE
     group = QUERY_HEADS // KEY_VALUE_HEADS
     scale = math.log2(math.e) / math.sqrt(HEAD_SIZE)
 
-    def attend(j):
-        at_rows = shard_rows(0, j)
+    T = B * rows
+    first_left = jnp.where(u > 1, 1, 0)
+    first_right = jnp.where(u < H - 2, H - 2, H - 1)
+
+    def clear():
+        peak[...] = jnp.full_like(peak, MASKED)
+        total[...] = jnp.zeros_like(total)
+
+    def visit(j, needed):
+        at_rows = shard_rows(j)
         first = (b * H + j) * rows
         pos = (first + lax.broadcasted_iota(jnp.int32, (rows, 1), 0)).astype(jnp.float32)
         lower = jnp.zeros((rows, 1), jnp.float32)
         for k in range(1, segments):
             lower = jnp.where(pos >= starts[k], starts[k], lower)
-        peak[...] = jnp.full_like(peak, MASKED)
-        total[...] = jnp.zeros_like(total)
-        tiles = (first + rows - 1) // T + 1
-
-        def key_tile(i, inner):
-            index = tiles - 1 - i
+
+        def key_tile(index):
             at_keys = pl.ds(pl.multiple_of(index * T, T), T)
-            key_pos = (index * T + lax.broadcasted_iota(jnp.int32, (rows, T), 1)).astype(
-                jnp.float32
-            )
+            key_pos = key_pos_ref[...] + (index * rows).astype(jnp.float32)
             bias = jnp.where((key_pos <= pos) & (key_pos >= lower), 0.0, MASKED)
             for g in range(groups):
                 keys = kv[at_keys, g * HEAD_SIZE : (g + 1) * HEAD_SIZE]
@@ -286,9 +262,19 @@
                 total[g] = total[g] * jnp.concatenate([decay, decay], axis=1) + jnp.dot(
                     shares, values, preferred_element_type=jnp.float32
                 )
+
+        def maybe(index, inner):
+            @pl.when(needed(index))
+            def _():
+                key_tile(index)
+
             return inner
 
-        lax.fori_loop(0, tiles, key_tile, 0)
+        lax.fori_loop(0, H, maybe, 0)
+
+    def conclude(j):
+        at_rows = shard_rows(j)
+        first = (b * H + j) * rows
         for h in range(groups * group):
             g, at = h // group, (h % group) * rows
             left[at_rows, h * HEAD_SIZE : (h + 1) * HEAD_SIZE] = (
@@ -303,10 +289,52 @@
         left[at_rows, qw : qw + HIDDEN] = high
         left[at_rows, qw + HIDDEN :] = (lows - high.astype(jnp.float32)).astype(jnp.bfloat16)
 
+    def phase(d, carry):
+        @pl.when((d == H - 1) & at_end)
+        def _():
+            await_keys(True)
+            clear()
+            visit(jnp.where(u == 0, first_right, first_left), lambda s: s != H - 1 - u)
+
+        @pl.when(d > 0)
+        def _():
+            for c in range(C):
+                @pl.when(u + d < H)
+                def _():
+                    send(u + d, c, 0).wait_recv()
+
+                    @pl.when(u > 0)
+                    def _():
+                        send(u + d, c, 0).start()
+
+                @pl.when(u - d >= 0)
+                def _():
+                    send(u - d, c, 1).wait_recv()
+
+                    @pl.when(u < H - 1)
+                    def _():
+                        send(u - d, c, 1).start()
+
+        def side_step(side, inner):
+            j = u + d * (1 - 2 * side)
+
+            @pl.when((j >= 0) & (j < H) & (d + 1 > side))
+            def _():
+                project(j)
+
+            return inner
+
+        lax.fori_loop(0, jnp.where(d > 0, 2, 1), side_step, 0)
+        return carry
+
+    lax.fori_loop(0, H, phase, 0)
+
+    await_keys(False)
+
     def own_part(j, c):
         columns = pl.ds(pl.multiple_of(c * width, width), width)
         return jnp.dot(
-            left[shard_rows(0, j), :], out_weights[:, columns], preferred_element_type=jnp.float32
+            left[shard_rows(j), :], out_weights[:, columns], preferred_element_type=jnp.float32
         )
 
     def hop(j, c, side):
@@ -327,6 +355,7 @@
 
     def place(n, side):
         p = n // D
+        p = jnp.where(p < 2, 1 - p, p)
         j = jnp.where(side == 0, p, H - 1 - p)
         sends = jnp.where(side == 0, u - j, j - u) > 0
         return j, n % D, sends
@@ -339,12 +368,22 @@
 
         def attend_side(side, side_carry):
             n, inside, _ = position(side)
-            j, c, sends = place(jnp.where(t == 0, 0, n), side)
-            due = (t == 0) | (inside & (c == 0) & (n > 0))
-
-            @pl.when(((t < final) & sends & due) | ((t == final) & (side == 0)))
-            def _():
-                attend(jnp.where(t == final, u, j))
+            j, c, sends = place(n, side)
+            started = jnp.where(side == 0, first_left, first_right)
+            opens = jnp.where(side == 0, u, H - 1 - u) > 0
+            due = inside & (c == 0) & sends & (j != started)
+
+            @pl.when(((t == 0) & opens) | ((t < final) & due) | ((t == final) & (side == 0)))
+            def _():
+                shard = jnp.where(t == 0, started, jnp.where(t == final, u, j))
+                resumed = (t == 0) & at_end
+
+                @pl.when(jnp.logical_not(resumed))
+                def _():
+                    clear()
+
+                visit(shard, lambda s: (s == H - 1 - u) | jnp.logical_not(resumed))
+                conclude(shard)
 
             return side_carry
 
@@ -454,17 +493,18 @@
     seg = segment_index.reshape(tokens // 128, 128)
     bf16 = jnp.bfloat16
     C, D = 3, 4
-    T = math.gcd(tokens, 1024)
+    key_pos = np.arange(B)[:, None] * block_rows + np.arange(rows)[None, :]
+    key_pos = jnp.asarray(key_pos.reshape(1, B * rows), jnp.float32)
     group_rows = QUERY_HEADS // KEY_VALUE_HEADS * rows
     groups = kw // HEAD_SIZE
     f32 = jnp.float32
     return pl.pallas_call(
-        functools.partial(block_kernel, H, B, C, D, T, segments),
+        functools.partial(block_kernel, H, B, C, D, segments),
         out_shape=jax.ShapeDtypeStruct((rows, features), bf16),
         in_specs=[IN_VMEM] * 2
         + [ANYWHERE] * 4
         + [IN_VMEM] * 3
-        + [ANYWHERE, IN_VMEM, ANYWHERE, IN_VMEM, IN_SMEM],
+        + [ANYWHERE, IN_VMEM, ANYWHERE, IN_VMEM, IN_VMEM, IN_SMEM],
         out_specs=IN_VMEM,
         scratch_shapes=[
             pltpu.VMEM((H, rows, features), bf16),
@@ -505,6 +545,7 @@
         output_down_maps,
         output_up_maps,
         seg,
+        key_pos,
         segment_adapter,
     )
 

time: 132 us -> 130 us (0.985)
  no operation moved by 1% of the time
where the time goes in v4:
time: 130 us
  Pallas kernels  128 us (98%)
  local copies, waits for them, and re-layouts  2.06 us (2%)
    pallas_call x1, Pallas kernels, shards(): pl.pallas_call(functools.partial(block_kernel, H, B, C, D, segments), out...  128 us

profile of v4, /device:TPU:15, one launch (start us, length us, event | category | flops | bytes accessed | tf_op | source)
XLA Modules:
  0.0 130.2 jit_solution(2626351594153068007)
XLA Ops:
  0.0 128.1 %attention_block.1 = bf16[96,4096]{1,0:T(8,128)(2,1)} custom-call(bf16[96,4096]{1,0:T(8,128)(2,1)} %x_ref.1, f32[1,4096]{1,0:T(1,128)} %bitcast.2, bf16[4096,384]{1,0:T(8,128)(2,1)} %down_ref.1, bf16[4096,1024]{1,0:T(8,128)(2,1)} %wq_ref.1, bf16[4096,256]{1,0:T(8,128)(2,1)} %wk_ref.1, bf16[4096,256]{1,0:T(8,128)(2,1)} %wv_ref.1, bf16[128,1024]{1,0:T(8,128)(2,1)} %uq_ref.1, ...), custom_call_target="tpu_custom_call" | custom-call | tf_op jit(solution)/shard_map/attention_block/pallas_call | solution.py:501
  128.1 2.1 %copy.17 = bf16[96,4096]{1,0:T(8,128)(2,1)} copy(bf16[96,4096]{1,0:T(8,128)(2,1)} %attention_block.1) | data formatting | bytes 1572864

commit v5 on v4

--- a/solution.py
+++ b/solution.py
@@ -92,9 +92,14 @@
     def _():
         pl.semaphore_signal(barrier, inc=1, device_id=(b, u + 1), device_id_type=MESH)
 
-    for d in range(1, B):
+    chips = B // 2
+    chip = b // 2
+    core = b % 2
+    sibling = b + 1 - 2 * core
+    pl.semaphore_signal(barrier, inc=1, device_id=(sibling, u), device_id_type=MESH)
+    for m in range(1, chips):
         pl.semaphore_signal(
-            barrier, inc=1, device_id=(lax.rem(b + d, B), u), device_id_type=MESH
+            barrier, inc=1, device_id=(lax.rem(b + 2 * m, B), u), device_id_type=MESH
         )
 
     def send(j, c, side):
@@ -127,11 +132,11 @@
 
     @pl.when((u > 0) & (u < H - 1))
     def _():
-        pl.semaphore_wait(barrier, B + 1)
+        pl.semaphore_wait(barrier, chips + 2)
 
     @pl.when((u == 0) | (u == H - 1))
     def _():
-        pl.semaphore_wait(barrier, B)
+        pl.semaphore_wait(barrier, chips + 1)
 
     send_if(u, 0)
     for c in range(1, C):
@@ -150,16 +155,38 @@
     def key_rows(block, j):
         return pl.ds(pl.multiple_of((j * B + block) * rows, rows), rows)
 
-    def kv_copy(j, d):
-        where = kv.at[key_rows(b, j), :]
+    def key_copy(block, j, sems, m, target):
+        where = kv.at[key_rows(block, j), :]
         return pltpu.make_async_remote_copy(
             src_ref=where,
             dst_ref=where,
-            send_sem=kv_send.at[d, j],
-            recv_sem=kv_recv.at[d, j],
-            device_id=(b + d, u),
+            send_sem=kv_send.at[sems, m, j],
+            recv_sem=kv_recv.at[sems, m, j],
+            device_id=(target, u),
             device_id_type=MESH,
         )
+
+    def far(j, m):
+        return key_copy(b, j, 0, m, b + 2 * m)
+
+    def near(j):
+        return key_copy(b, j, 0, 0, sibling)
+
+    def passed(j, m):
+        return key_copy(b - 2 * m, j, 1, m, sibling)
+
+    def relay(d):
+        def relay_side(side, carry):
+            j = u + d * (1 - 2 * side)
+            for m in range(1, chips):
+                @pl.when((j >= 0) & (j < H) & (d + 1 > side) & (chip - m >= 0))
+                def _():
+                    far(j, m).wait_recv()
+                    passed(j, m).start()
+
+            return carry
+
+        lax.fori_loop(0, jnp.where(d > 0, 2, 1), relay_side, 0)
 
     def project(j):
         shard = rows_buf[j]
@@ -183,10 +210,14 @@
 
         kv[key_rows(b, j), :kw] = product(0, kw, lowered(1), uk_ref[...])
         kv[key_rows(b, j), kw:] = product(kw, kw, lowered(2), uv_ref[...])
-        for d in range(1, B):
-            @pl.when(b + d < B)
-            def _():
-                kv_copy(j, d).start()
+        for m in range(1, chips):
+            @pl.when(chip + m < chips)
+            def _():
+                far(j, m).start()
+
+        @pl.when(core == 0)
+        def _():
+            near(j).start()
 
         low = lowered(0)
         step = 256
@@ -205,10 +236,15 @@
     def await_keys(known):
         def keys_arrived(j, carry):
             early = at_end & (j != H - 1 - u)
-            for d in range(1, B):
-                @pl.when((b - d >= 0) & (early if known else jnp.logical_not(early)))
+            due = early if known else jnp.logical_not(early)
+            for m in range(1, chips):
+                @pl.when((chip - m >= 0) & due)
                 def _():
-                    kv_copy(j, d).wait_recv()
+                    passed(j, m).wait_recv()
+
+            @pl.when((core == 1) & due)
+            def _():
+                near(j).wait_recv()
 
             return carry
 
@@ -290,6 +326,10 @@
         left[at_rows, qw + HIDDEN :] = (lows - high.astype(jnp.float32)).astype(jnp.bfloat16)
 
     def phase(d, carry):
+        @pl.when((d > 0) & at_end)
+        def _():
+            relay(d - 1)
+
         @pl.when((d == H - 1) & at_end)
         def _():
             await_keys(True)
@@ -315,6 +355,10 @@
                     def _():
                         send(u - d, c, 1).start()
 
+        @pl.when((d > 0) & jnp.logical_not(at_end))
+        def _():
+            relay(d - 1)
+
         def side_step(side, inner):
             j = u + d * (1 - 2 * side)
 
@@ -329,6 +373,7 @@
 
     lax.fori_loop(0, H, phase, 0)
 
+    relay(H - 1)
     await_keys(False)
 
     def own_part(j, c):
@@ -446,10 +491,18 @@
             def _():
                 send(j, c, 1).wait_send()
 
-        for d in range(1, B):
-            @pl.when(b + d < B)
-            def _():
-                kv_copy(j, d).wait_send()
+        for m in range(1, chips):
+            @pl.when(chip + m < chips)
+            def _():
+                far(j, m).wait_send()
+
+            @pl.when(chip - m >= 0)
+            def _():
+                passed(j, m).wait_send()
+
+        @pl.when(core == 0)
+        def _():
+            near(j).wait_send()
 
         for c in range(D):
             @pl.when(j != u)
@@ -522,8 +575,8 @@
             pltpu.SemaphoreType.DMA((3,)),
             pltpu.SemaphoreType.DMA((2, H, C)),
             pltpu.SemaphoreType.DMA((H, C)),
-            pltpu.SemaphoreType.DMA((B, H)),
-            pltpu.SemaphoreType.DMA((B, H)),
+            pltpu.SemaphoreType.DMA((2, B // 2, H)),
+            pltpu.SemaphoreType.DMA((2, B // 2, H)),
             pltpu.SemaphoreType.DMA((H, D)),
             pltpu.SemaphoreType.DMA((2, H, D)),
         ],

time: 130 us -> 126 us (0.969)
  Pallas kernels: 128 us -> 124 us
    pallas_call x1, Pallas kernels: 128 us -> 124 us  [shards(): pl.pallas_call(functools.partial(block_kernel, H, B, C, D, segments), out...]
where the time goes in v5:
time: 126 us
  Pallas kernels  124 us (98%)
  local copies, waits for them, and re-layouts  2.06 us (2%)
    pallas_call x1, Pallas kernels, shards(): pl.pallas_call(functools.partial(block_kernel, H, B, C, D, segments), out...  124 us

profile of v5, /device:TPU:15, one launch (start us, length us, event | category | flops | bytes accessed | tf_op | source)
XLA Modules:
  0.0 125.7 jit_solution(9767409685462436368)
XLA Ops:
  0.0 123.6 %attention_block.1 = bf16[96,4096]{1,0:T(8,128)(2,1)} custom-call(bf16[96,4096]{1,0:T(8,128)(2,1)} %x_ref.1, f32[1,4096]{1,0:T(1,128)} %bitcast.2, bf16[4096,384]{1,0:T(8,128)(2,1)} %down_ref.1, bf16[4096,1024]{1,0:T(8,128)(2,1)} %wq_ref.1, bf16[4096,256]{1,0:T(8,128)(2,1)} %wk_ref.1, bf16[4096,256]{1,0:T(8,128)(2,1)} %wv_ref.1, bf16[128,1024]{1,0:T(8,128)(2,1)} %uq_ref.1, ...), custom_call_target="tpu_custom_call" | custom-call | tf_op jit(solution)/shard_map/attention_block/pallas_call | solution.py:554
  123.6 2.1 %copy.17 = bf16[96,4096]{1,0:T(8,128)(2,1)} copy(bf16[96,4096]{1,0:T(8,128)(2,1)} %attention_block.1) | data formatting | bytes 1572864

commit v6 on v5

--- a/solution.py
+++ b/solution.py
@@ -21,7 +21,7 @@
 MESH = pl.DeviceIdType.MESH
 VMEM_LIMIT = 60 * 1024 * 1024
 MASKED = -1e30
-LAG = 2
+LAG = 4
 
 
 def segment_starts(seg_ref, segments):
@@ -545,7 +545,7 @@
     block_rows = rows * H
     seg = segment_index.reshape(tokens // 128, 128)
     bf16 = jnp.bfloat16
-    C, D = 3, 4
+    C, D = 3, 8
     key_pos = np.arange(B)[:, None] * block_rows + np.arange(rows)[None, :]
     key_pos = jnp.asarray(key_pos.reshape(1, B * rows), jnp.float32)
     group_rows = QUERY_HEADS // KEY_VALUE_HEADS * rows

time: 126 us -> 128 us (1.016)
    pallas_call x1, Pallas kernels: 124 us -> 125 us  [shards(): pl.pallas_call(functools.partial(block_kernel, H, B, C, D, segments), out...]
where the time goes in v6:
time: 128 us; the launch traced here: 127 us
  Pallas kernels  125 us (98%)
  local copies, waits for them, and re-layouts  2.06 us (2%)
    pallas_call x1, Pallas kernels, shards(): pl.pallas_call(functools.partial(block_kernel, H, B, C, D, segments), out...  125 us

profile of v6, /device:TPU:15, one launch (start us, length us, event | category | flops | bytes accessed | tf_op | source)
XLA Modules:
  0.0 127.1 jit_solution(17980341218533740421)
XLA Ops:
  0.0 125.0 %attention_block.1 = bf16[96,4096]{1,0:T(8,128)(2,1)} custom-call(bf16[96,4096]{1,0:T(8,128)(2,1)} %x_ref.1, f32[1,4096]{1,0:T(1,128)} %bitcast.2, bf16[4096,384]{1,0:T(8,128)(2,1)} %down_ref.1, bf16[4096,1024]{1,0:T(8,128)(2,1)} %wq_ref.1, bf16[4096,256]{1,0:T(8,128)(2,1)} %wk_ref.1, bf16[4096,256]{1,0:T(8,128)(2,1)} %wv_ref.1, bf16[128,1024]{1,0:T(8,128)(2,1)} %uq_ref.1, ...), custom_call_target="tpu_custom_call" | custom-call | tf_op jit(solution)/shard_map/attention_block/pallas_call | solution.py:554
  125.0 2.1 %copy.17 = bf16[96,4096]{1,0:T(8,128)(2,1)} copy(bf16[96,4096]{1,0:T(8,128)(2,1)} %attention_block.1) | data formatting | bytes 1572864
